TPU v7x, 512 devices: a whole 4x4x16 slice. The times are simulated.
512 devices in a mesh: ctx: 32 (over z, core), tp: 4 (over y), dp: 4 (over x).
Axes of the slice: x: 4, y: 4, z: 16, core: 2. Of those that a mesh axis runs over, the one named last changes fastest.
Arguments:
- q_raw: bfloat16 [4, 4096, 4096], P('dp', 'ctx', 'tp'), may hold values from -30 to 30
- k_raw: bfloat16 [4, 4096, 512], P('dp', 'ctx', 'tp'), may hold values from -30 to 30
- values_in: bfloat16 [4, 4096, 512], P('dp', 'ctx', 'tp'), may hold values from -6 to 6
- grad_out: bfloat16 [4, 4096, 4096], P('dp', 'ctx', 'tp'), may hold values from -15 to 15
- q_gain: float32 [128], replicated, may hold values from 0.5 to 5.5
- k_gain: float32 [128], replicated, may hold values from 0.5 to 5.5
Outputs:
- d_q: bfloat16 [4, 4096, 4096], P('dp', 'ctx', 'tp')
- d_k: bfloat16 [4, 4096, 512], P('dp', 'ctx', 'tp')
- d_v: bfloat16 [4, 4096, 512], P('dp', 'ctx', 'tp')
- gain_grads: float32 [2, 128], replicated
All inputs are finite; a program needn't handle non-finite values.
Results may differ from a plain program's by a relative error of at most 0.009.
The roundings to bfloat16 on the way count: a program that leaves them out, or rounds other values in their place, can miss the bound.
Values may be sent and summed in bfloat16 or wider, within the bound.
A program may use at most 64 MiB of HBM per device.

v0:
```python
import jax
import jax.numpy as jnp
from jax import lax
from jax.sharding import PartitionSpec as P

KEY_BLOCK = 512


eps = 1e-06
masked = -1e30


def normalize(raw, gain, head_width):
    values = raw.astype(jnp.float32).reshape(raw.shape[0], -1, head_width)
    inverse = lax.rsqrt(jnp.mean(values * values, axis=2, keepdims=True) + eps)
    return (values, inverse, (values * inverse * gain).astype(jnp.bfloat16))


def norm_back(values, inverse, gain, upstream):
    scaled = gain * upstream
    inner = jnp.mean(scaled * values, axis=2, keepdims=True)
    grad_in = inverse * scaled - values * (inverse * inverse * inverse) * inner
    gain_part = jnp.sum(upstream * values * inverse, axis=(0, 1))
    return (grad_in, gain_part)


def score_block(queries, cotans, keys_tile, vals_tile, query_positions, offset, score_scale):
    scores = jnp.dot(queries, keys_tile.T, preferred_element_type=jnp.float32) * score_scale
    key_positions = offset + jnp.arange(keys_tile.shape[0], dtype=jnp.int32)
    allowed = key_positions[None, :] <= query_positions[:, None]
    scores = jnp.where(allowed, scores, masked)
    dprob = jnp.dot(cotans, vals_tile.T, preferred_element_type=jnp.float32)
    return (scores, dprob, allowed)


def block_grads(
    queries, cotans, keys_tile, vals_tile, query_positions, offset, score_scale, lse, delta
):
    scores, dprob, allowed = score_block(
        queries, cotans, keys_tile, vals_tile, query_positions, offset, score_scale
    )
    prob = jnp.where(allowed, jnp.exp(scores - lse[:, None]), 0.0)
    dscore = prob * (dprob - delta[:, None])
    return (prob.astype(jnp.bfloat16), dscore.astype(jnp.bfloat16))


def shards(q_raw, k_raw, values_in, grad_out, q_gain, k_gain):
    head_width = q_gain.shape[0]
    row_count = q_raw.shape[1]
    q_vals, q_inv, q_norm = normalize(q_raw[0], q_gain, head_width)
    local_heads = q_vals.shape[1]
    k_vals, k_inv, k_norm = normalize(k_raw[0], k_gain, head_width)
    upstream = grad_out[0]
    q_flat = q_norm.reshape(row_count, local_heads * head_width)
    ctx_place = lax.axis_index("ctx")
    query_positions = ctx_place * row_count + jnp.arange(row_count, dtype=jnp.int32)
    flat_rows = row_count * local_heads
    queries = q_flat.reshape(flat_rows, head_width)
    cotans = upstream.reshape(flat_rows, head_width)
    row_positions = jnp.repeat(query_positions, local_heads)
    keys_all, vals_all = (
        lax.all_gather(k_norm.reshape(row_count, head_width), "ctx", axis=0, tiled=True),
        lax.all_gather(values_in[0], "ctx", axis=0, tiled=True),
    )
    total_keys = keys_all.shape[0]
    block_len = min(KEY_BLOCK, total_keys)
    num_blocks = total_keys // block_len
    key_tiles = keys_all.reshape(num_blocks, block_len, head_width)
    val_tiles = vals_all.reshape(num_blocks, block_len, head_width)
    last_query = jnp.max(query_positions)
    score_scale = head_width ** (-0.5)

    def first_pass(carry, block_index):
        offset = block_index * block_len

        def first_active(operand):
            running_max, row_mass, weighted = carry
            scores, dprob, allowed = score_block(
                queries,
                cotans,
                key_tiles[block_index],
                val_tiles[block_index],
                row_positions,
                offset,
                score_scale,
            )
            new_max = jnp.maximum(running_max, jnp.max(scores, axis=1))
            shrink = jnp.exp(running_max - new_max)
            prob = jnp.where(allowed, jnp.exp(scores - new_max[:, None]), 0.0)
            return (
                new_max,
                row_mass * shrink + jnp.sum(prob, axis=1),
                weighted * shrink + jnp.sum(prob * dprob, axis=1),
            )

        def first_skipped(operand):
            return carry

        return (lax.cond(offset <= last_query, first_active, first_skipped, None), None)

    start_state = (
        jnp.full((flat_rows,), masked, jnp.float32),
        jnp.zeros((flat_rows,), jnp.float32),
        jnp.zeros((flat_rows,), jnp.float32),
    )
    (running_max, row_mass, weighted), unused = lax.scan(
        first_pass, start_state, jnp.arange(num_blocks, dtype=jnp.int32)
    )
    lse = running_max + jnp.log(row_mass)
    delta = weighted / row_mass
    zero_queries = jnp.zeros((flat_rows, head_width), jnp.float32)

    def second_pass(accum, block_index):
        offset = block_index * block_len

        def second_active(operand):
            prob_b, dscore_b = block_grads(
                queries,
                cotans,
                key_tiles[block_index],
                val_tiles[block_index],
                row_positions,
                offset,
                score_scale,
                lse,
                delta,
            )
            grad_keys = jnp.dot(dscore_b.T, queries, preferred_element_type=jnp.float32)
            grad_vals = jnp.dot(prob_b.T, cotans, preferred_element_type=jnp.float32)
            updated = accum + jnp.dot(
                dscore_b, key_tiles[block_index], preferred_element_type=jnp.float32
            )
            return (updated, jnp.concatenate([grad_keys, grad_vals], axis=1))

        def second_skipped(operand):
            return (accum, jnp.zeros((block_len, 2 * head_width), jnp.float32))

        return lax.cond(offset <= last_query, second_active, second_skipped, None)

    query_accum, key_tiles_out = lax.scan(
        second_pass, zero_queries, jnp.arange(num_blocks, dtype=jnp.int32)
    )
    key_parts = lax.psum_scatter(
        key_tiles_out.reshape(total_keys, 2 * head_width), "ctx", scatter_dimension=0, tiled=True
    )
    query_grads = (score_scale * query_accum).reshape(row_count, local_heads * head_width)
    q_grad, q_part = norm_back(
        q_vals, q_inv, q_gain, query_grads.reshape(row_count, local_heads, head_width)
    )
    key_upstream = (score_scale * key_parts[:, :head_width]).reshape(row_count, 1, head_width)
    k_grad, k_part = norm_back(k_vals, k_inv, k_gain, key_upstream)
    value_grads = key_parts[:, head_width:]
    q_total, k_total = lax.psum((q_part, k_part), ("ctx", "tp", "dp"))
    d_q = q_grad.reshape(row_count, local_heads * head_width).astype(jnp.bfloat16)[None]
    d_k = k_grad.reshape(row_count, head_width).astype(jnp.bfloat16)[None]
    d_v = value_grads.astype(jnp.bfloat16)[None]
    return (d_q, d_k, d_v, jnp.stack([q_total, k_total]))


def solution(mesh):
    return jax.shard_map(
        shards,
        mesh=mesh,
        in_specs=(
            P("dp", "ctx", "tp"),
            P("dp", "ctx", "tp"),
            P("dp", "ctx", "tp"),
            P("dp", "ctx", "tp"),
            P(),
            P(),
        ),
        out_specs=(P("dp", "ctx", "tp"), P("dp", "ctx", "tp"), P("dp", "ctx", "tp"), P()),
        check_vma=False,
    )
```

profile of v0, /device:TPU:1, one launch (start us, length us, event | category | flops | bytes accessed | tf_op | source)
XLA Modules:
  0.0 524.1 jit_solution(4893946606852159550)
XLA Ops:
  7.2 0.9 fusion.40
  8.1 1.5 fusion.33
  9.7 0.7 all-gather.6.cloned.1.call-update
  10.5 1.1 reshape.216
  11.5 1.0 multiply_bitcast_fusion
  12.6 0.2 reduce_sum.72
  13.1 0.6 iota_add_fusion.2
  13.7 0.2 multiply_convert_fusion
  13.9 73.2 %all-gather.4.cloned.1.call-done = bf16[4096,128]{1,0:T(8,128)(2,1)} async-done(((bf16[128,128]{1,0:T(8,128)(2,1)}), bf16[4096,128]{1,0:T(8,128)(2,1)}) %all-gather.4.cloned.1.call-update) | async-done | bytes 1048592 | tf_op jit(solution)/shard_map/all_gather | solution.py:62
  87.1 70.0 %all-gather.6.cloned.1.call-done = bf16[1,4096,128]{2,1,0:T(8,128)(2,1)} async-done(((bf16[1,128,128]{2,1,0:T(8,128)(2,1)}), bf16[1,4096,128]{2,1,0:T(8,128)(2,1)}) %all-gather.6.cloned.1.call-update) | async-done | bytes 1048592 | tf_op jit(solution)/shard_map/all_gather | solution.py:63
  157.1 21.3 %while.31 = (s32[]{:T(128)}, f32[1024]{0:T(1024)S(1)}, f32[1024]{0:T(1024)S(1)}, f32[1024]{0:T(1024)S(1)}, s32[8]{0:T(128)S(1)}, /*index=5*/s32[]{:T(128)}, bf16...) while((s32[]{:T(128)}, f32[1024]{0:T(1024)S(1)}, ...), condition=%wide.region_9.10_spmd.clone, body=%wide.region_3.9_spmd.clone.sunk | while | flops 277351936 | bytes 7185241 | solution.py:106
  157.1 0.6 dynamic_slice.46
  159.0 5.9 %conditional.6 = ((f32[1024]{0:T(1024)S(1)}, f32[1024]{0:T(1024)S(1)}, f32[1024]{0:T(1024)S(1)})) conditional(s32[]{:T(128)} %convert_element_type.129, (f32[1024]{0:T(1024)S(1)}, f32[1024]{0:T(1024)S(1)}, f32[1024]{0:T(1024)S(1)}) %tuple.72, (s32[]{:T(128)}, s32[128]{0:T(128)S(1)}, s32[]{:T(128)}, bf16[8,512,128]{2,1,0:T(8,128)(2,1)}, ...), branch_computations={%region_4.4_spmd, %region_5.8_spmd} | conditional | flops 277351936 | bytes 7184974 | solution.py:99
  161.1 1.4 fusion.5
  162.5 0.6 fusion.6
  163.2 1.7 fusion.4
  164.9 0.6 dynamic_slice.46
  166.8 0.6 dynamic_slice.46
  168.7 0.6 dynamic_slice.46
  170.7 0.6 dynamic_slice.46
  172.6 0.6 dynamic_slice.46
  174.5 0.6 dynamic_slice.46
  176.4 0.6 dynamic_slice.46
  178.4 31.6 %while.32 = (s32[]{:T(128)}, f32[1024,128]{1,0:T(8,128)S(1)}, f32[8,512,256]{2,1,0:T(8,128)}, s32[8]{0:T(128)S(1)}, s32[]{:T(128)}, /*index=5*/bf16[8,512,128]{2...) while((s32[]{:T(128)}, f32[1024,128]{1,0:T(8,128)S(1)}, ...), condition=%wide.region_13.14_spmd.clone, body=%wide.region_10.13_spmd.clone.sunk | while | flops 676069888 | bytes 15627581 | solution.py:140
  178.4 0.6 dynamic_slice.47
  180.3 7.5 %conditional.7 = (f32[1024,128]{1,0:T(8,128)S(1)}, f32[1,512,256]{1,2,0:T(8,128)S(1)}) conditional(s32[]{:T(128)} %convert_element_type.130, f32[1024,128]{1,0:T(8,128)S(1)} %get-tuple-element.542, (s32[]{:T(128)}, s32[128]{0:T(128)S(1)}, s32[]{:T(128)}, bf16[8,512,128]{2,1,0:T(8,128)(2,1)}, bf16[1024,128]{1,0:T(8,128)(2,1)S(1)}, ...), branch_computations={%region_11.11_spmd, %region_12.12_spmd} | conditional | flops 676069888 | bytes 13529666 | solution.py:138
  182.5 1.6 compare_select_fusion.2
  184.1 1.3 fusion.16
  185.4 0.5 fusion.45
  185.9 0.5 fusion.17
  186.4 1.4 convolution_add_fusion
  187.9 0.2 copy.22
  188.1 0.8 constant_dynamic-update-slice_fusion.2
  188.9 0.6 dynamic_slice.47
  190.9 0.2 copy.22
  191.1 0.8 constant_dynamic-update-slice_fusion.2
  191.9 0.6 dynamic_slice.47
  193.9 0.2 copy.22
  194.1 0.9 constant_dynamic-update-slice_fusion.2
  195.0 0.6 dynamic_slice.47
  196.9 0.2 copy.22
  197.1 0.9 constant_dynamic-update-slice_fusion.2
  198.0 0.6 dynamic_slice.47
  200.0 0.2 copy.22
  200.2 0.8 constant_dynamic-update-slice_fusion.2
  201.0 0.6 dynamic_slice.47
  203.0 0.2 copy.22
  203.2 0.9 constant_dynamic-update-slice_fusion.2
  204.0 0.6 dynamic_slice.47
  206.0 0.2 copy.22
  206.2 0.8 constant_dynamic-update-slice_fusion.2
  207.0 0.6 dynamic_slice.47
  209.0 0.2 copy.22
  209.2 0.9 constant_dynamic-update-slice_fusion.2
  210.1 0.2 mul.278
  210.4 0.2 mul.299
  210.7 0.4 multiply_reduce_fusion
  211.7 0.9 subtract_convert_fusion
  212.6 194.2 %reduce-scatter.2.cloned.1.call-done = f32[128,256]{1,0:T(8,128)} async-done(((f32[4096,256]{1,0:T(8,128)}), f32[128,256]{1,0:T(8,128)}) %reduce-scatter.2.cloned.1.call-update) | async-done | bytes 131088 | tf_op jit(solution)/shard_map/reduce_scatter | solution.py:143
  406.8 1.0 fusion.39
  407.8 106.1 %all-reduce = (f32[1,128]{1,0:T(1,128)S(1)}, f32[1,128]{1,0:T(1,128)S(1)}) all-reduce(f32[1,128]{1,0:T(1,128)S(1)} %bitcast.100, f32[1,128]{1,0:T(1,128)S(1)} %bitcast.99), channel_id=1, replica_groups=mesh['ctx'=32,'tp'=4,'dp'=4] {'ctx','tp','dp'}, use_global_device_ids=true, to_apply=%region_20.21 | all-reduce | flops 256 | bytes 2048 | tf_op jit(solution)/shard_map/psum | solution.py:153
  514.0 0.6 pad_maximum_fusion
  514.5 1.5 fusion.41
  516.0 1.6 fusion.42
  (70 shorter events, 2.7 us)
Async XLA Ops:
  7.2 5.8 %copy-start.2 = (bf16[1,128,1024]{2,1,0:T(8,128)(2,1)S(1)}, bf16[1,128,1024]{2,1,0:T(8,128)(2,1)}, u32[]{:S(2)}) copy-start(bf16[1,128,1024]{2,1,0:T(8,128)(2,1)} %param.17) | copy-start | bytes 786436
  7.2 6.6 %copy-start.3 = (f32[128]{0:T(128)S(1)}, f32[128]{0:T(128)}, u32[]{:S(2)}) copy-start(f32[128]{0:T(128)} %param.18) | copy-start | bytes 1540
  7.2 79.9 %all-gather.4.cloned.1.call-start = ((), (), s32[]{:S(2)}) async-start(), calls=%async_computation.1 | async-start | bytes 1081344 | tf_op jit(solution)/shard_map/all_gather | solution.py:62
  9.6 147.4 %all-gather.6.cloned.1.call-start = ((), (), s32[]{:S(2)}) async-start(), calls=%async_computation.3 | async-start | bytes 1081344 | tf_op jit(solution)/shard_map/all_gather | solution.py:63
  10.4 396.4 %reduce-scatter.2.cloned.1.call-start = ((), (), s32[]{:S(2)}) async-start(), calls=%async_computation.2 | async-start | bytes 4325376 | tf_op jit(solution)/shard_map/reduce_scatter | solution.py:143
  210.1 0.7 copy-start.4
  210.7 0.9 copy-start
  211.5 195.3 %copy-start.1 = (bf16[1,128,128]{2,1,0:T(8,128)(2,1)S(1)}, bf16[1,128,128]{2,1,0:T(8,128)(2,1)}, u32[]{:S(2)}) copy-start(bf16[1,128,128]{2,1,0:T(8,128)(2,1)} %param.15) | copy-start | bytes 98308
Sparse Core Ops, SparseCore 0:
  10.7 76.3 all-gather.3
  89.2 67.8 all-gather.5
  210.2 196.5 reduce-scatter.1
where the time goes:
time: 526 us; the launch traced here: 524 us
  waiting for transfers between devices  338 us (64%)
  blocking collectives  106 us (20%)
  loops' own time  25.5 us (5%)
  local copies, waits for them, and re-layouts  22.4 us (4%)
  between operations  14 us (3%)
  other arithmetic  9.55 us (2%)
  matrix products  8.35 us (2%)
    reduce_scatter x1, waiting for transfers between devices, shards(): lax.psum_scatter(key_tiles_out.reshape(total_keys, 2 * head_width), 'ctx'...  194 us
    psum x1, blocking collectives, shards(): q_total, k_total = lax.psum((q_part, k_part), ('ctx', 'tp', 'dp'))  106 us
    all_gather x1, waiting for transfers between devices, shards(): lax.all_gather(k_norm.reshape(row_count, head_width), 'ctx', axis=0, tile...  73.2 us
    all_gather x1, waiting for transfers between devices, shards(): lax.all_gather(values_in[0], 'ctx', axis=0, tiled=True)  70 us
    another operation x1, loops' own time, shards(): lax.scan(first_pass, start_state, jnp.arange(num_blocks, dtype=jnp.int32))  10.6 us
    another operation x1, loops' own time, shards(): lax.scan(second_pass, zero_queries, jnp.arange(num_blocks, dtype=jnp.int32))  10.6 us
  transfers between devices with their start and end apart: 3, of which 3 were waited for; matrix products, arithmetic and copies ran while one was open for 1% of the time, Pallas kernels for 0%

commit v1 on v0

v1 whole, which is shorter than its diff:
```python
import functools
import math

import jax
import jax.numpy as jnp
from jax import lax
from jax.experimental import pallas as pl
from jax.experimental.pallas import tpu as pltpu
from jax.sharding import PartitionSpec as P

HD = 128
CW = 256
EPS = 1e-06
MASKED = -1e30
F32 = jnp.float32
BF16 = jnp.bfloat16
MESH = pl.DeviceIdType.MESH


def dot(a, b, contract):
    return lax.dot_general(
        a, b, (((contract[0],), (contract[1],)), ((), ())), preferred_element_type=F32
    )


def inverse_rms(x):
    return lax.rsqrt(jnp.mean(x * x, axis=1, keepdims=True) + EPS)


def norm_back(x, inv, gain, upstream):
    scaled = gain * upstream
    inner = jnp.mean(scaled * x, axis=1, keepdims=True)
    grad = inv * scaled - x * (inv * inv * inv) * inner
    return grad, jnp.sum(upstream * x * inv, axis=0, keepdims=True)


def first_pass(kv, qh, go, probs, dprobs, block_max, stats, zo, core, diagonal, scale2):
    keys = kv[pl.ds(2 * zo, 2), 0].reshape(2 * HD, HD)
    vals = kv[pl.ds(2 * zo, 2), 1].reshape(2 * HD, HD)
    total = qh.shape[0]
    for start in range(0, total, CW):
        cols = slice(start, start + CW)
        s = dot(keys, qh[cols, :], (1, 1))
        if diagonal:
            key_pos = lax.broadcasted_iota(jnp.int32, (2 * HD, CW), 0)
            query_pos = core * HD + lax.broadcasted_iota(jnp.int32, (2 * HD, CW), 1) % HD
            s = jnp.where(key_pos <= query_pos, s, MASKED)
        dp = dot(vals, go[cols, :], (1, 1))
        top = jnp.max(s, axis=0, keepdims=True)
        if not diagonal:
            old = stats[0:1, cols]
            top = jnp.maximum(top, old)
        p = jnp.exp2(s * scale2 - top * scale2)
        mass = jnp.sum(p, axis=0, keepdims=True)
        weighted = jnp.sum(p * dp, axis=0, keepdims=True)
        if not diagonal:
            shrink = jnp.exp2((old - top) * scale2)
            mass += stats[1:2, cols] * shrink
            weighted += stats[2:3, cols] * shrink
        stats[0:1, cols] = top
        stats[1:2, cols] = mass
        stats[2:3, cols] = weighted
        block_max[zo, :, cols] = top
        probs[zo, :, cols] = p
        dprobs[zo, :, cols] = dp


def second_pass(kv, qh, go, probs, dprobs, block_max, stats, prob_b, dscore_b, dq_t, sums, zo, scale2):
    total = qh.shape[0]
    keys = kv[pl.ds(2 * zo, 2), 0].reshape(2 * HD, HD)
    for start in range(0, total, CW):
        cols = slice(start, start + CW)
        factor = jnp.exp2((block_max[zo, :, cols] - stats[0:1, cols]) * scale2) * stats[1:2, cols]
        p = probs[zo, :, cols] * factor
        ds = p * (dprobs[zo, :, cols] - stats[2:3, cols])
        prob_b[:, cols] = p.astype(BF16)
        ds = ds.astype(BF16)
        dscore_b[:, cols] = ds
        dq_t[:, cols] += dot(keys, ds, (0, 0))
    sums[0] = dot(dscore_b[...], qh[...], (1, 0)).reshape(2, HD, HD)
    sums[1] = dot(prob_b[...], go[...], (1, 0)).reshape(2, HD, HD)


def kernel(
    n, tp, dp,
    q_hbm, k_hbm, v_hbm, g_hbm, q_gain, k_gain,
    dq_hbm, dk_out, dv_out, gains_out,
    q_raw, k_raw, qh, go, kv, probs, dprobs, block_max, stats, prob_b, dscore_b, dq_t, dq_out,
    keep, swap_out, swap_in, ring_out, ring_in, line_out, line_in, plane_out, plane_in,
    load_sem, head_sem, store_sem,
    g_send, g_recv, sib_send, sib_recv, r_send, r_recv, swap_send, swap_recv,
    line_send, line_recv, plane_send, plane_recv,
):
    chips, half, heads = n // 2, n // 4, qh.shape[0] // HD
    scale = HD ** (-0.5)
    scale2 = scale * math.log2(math.e)
    me = lax.axis_index("ctx")
    z, core = me // 2, me % 2
    sibling = me + 1 - 2 * core
    place = lax.axis_index("tp") * dp + lax.axis_index("dp")
    group = tp * dp

    barrier = pltpu.get_barrier_semaphore()

    @pl.loop(1, n)
    def _(i):
        pl.semaphore_signal(barrier, 1, device_id={"ctx": (me + i) % n}, device_id_type=MESH)

    @pl.loop(1, group)
    def _(i):
        to = (place + i) % group
        pl.semaphore_signal(barrier, 1, device_id={"tp": to // dp, "dp": to % dp}, device_id_type=MESH)

    def load(i):
        src, dst = ((k_hbm.at[0], k_raw), (v_hbm.at[0], kv.at[me, 1]), (q_hbm.at[0], q_raw))[i]
        return pltpu.make_async_copy(src, dst, load_sem.at[i])

    def load_head(h):
        return pltpu.make_async_copy(
            g_hbm.at[0, :, pl.ds(h * HD, HD)], go.at[pl.ds(h * HD, HD)], head_sem.at[h]
        )

    for i in range(3):
        load(i).start()
    for h in range(heads):
        load_head(h).start()

    load(0).wait()
    x = k_raw[...].astype(F32)
    kv[me, 0] = (x * inverse_rms(x) * k_gain[...]).astype(BF16)
    load(1).wait()

    def ring_copy(direction, owner, index, part, to):
        block = kv.at[2 * owner + core, part]
        return pltpu.make_async_remote_copy(
            block, block, g_send.at[direction, index, part], g_recv.at[direction, index, part],
            device_id={"ctx": 2 * to + core}, device_id_type=MESH,
        )

    def sibling_copy(owner, part, owner_core):
        block = kv.at[2 * owner + owner_core, part]
        return pltpu.make_async_remote_copy(
            block, block, sib_send.at[owner, part], sib_recv.at[owner, part],
            device_id={"ctx": sibling}, device_id_type=MESH,
        )

    pl.semaphore_wait(barrier, n + group - 2)

    first_up = z < chips - 1
    first_around = z <= half - 2
    for part in range(2):
        @pl.when(first_up)
        def _():
            ring_copy(0, z, 0, part, z + 1).start()

        @pl.when(first_around)
        def _():
            ring_copy(1, z, z, part, chips - 1).start()

        sibling_copy(z, part, core).start()

    load(2).wait()
    for h in range(heads):
        cols = slice(h * HD, (h + 1) * HD)
        x = q_raw[:, cols].astype(F32)
        qh[cols, :] = (x * inverse_rms(x) * q_gain[...]).astype(BF16)
    for h in range(heads):
        load_head(h).wait()

    one = functools.partial(
        first_pass, kv, qh, go, probs, dprobs, block_max, stats, core=core, scale2=scale2
    )
    two = functools.partial(
        second_pass, kv, qh, go, probs, dprobs, block_max, stats, prob_b, dscore_b, dq_t, scale2=scale2
    )

    for part in range(2):
        sibling_copy(z, part, 1 - core).wait_recv()
    one(zo=z, diagonal=True)

    def gathered(direction, step):
        owner = jnp.where(direction == 0, z - 1 - step, step)
        limit = jnp.where(direction == 0, z, z - half)
        return owner, step < limit

    def forwarded(direction, step):
        to = jnp.where(direction == 0, z + 1, z - 1)
        index = jnp.where(direction == 0, step + 1, step)
        limit = jnp.where(direction == 0, jnp.where(z < chips - 1, half - 1, 0), z - half - 1)
        return to, index, step < limit

    @pl.loop(0, half + 1)
    def _(step):
        @pl.when(step < half)
        def _():
            @pl.loop(0, 2)
            def _(direction):
                owner, comes = gathered(direction, step)
                to, index, goes = forwarded(direction, step)

                @pl.when(comes)
                def _():
                    for part in range(2):
                        ring_copy(direction, owner, step, part, to).wait_recv()

                        @pl.when(goes)
                        def _():
                            ring_copy(direction, owner, index, part, to).start()

                        sibling_copy(owner, part, core).start()

        @pl.when(step >= 1)
        def _():
            @pl.loop(0, 2)
            def _(direction):
                owner, comes = gathered(direction, step - 1)

                @pl.when(comes)
                def _():
                    for part in range(2):
                        sibling_copy(owner, part, 1 - core).wait_recv()
                    one(zo=owner, diagonal=False)

    inv_mass = 1.0 / stats[1:2, :]
    stats[2:3, :] = stats[2:3, :] * inv_mass
    stats[1:2, :] = inv_mass
    dq_t[...] = jnp.zeros_like(dq_t)

    def owed(direction, step):
        owner = jnp.where(direction == 0, z - half + step, z - half - 1 - step)
        last = jnp.where(direction == 0, half, half - 2)
        return owner, jnp.logical_and(owner >= 0, step <= last)

    def swap(owner):
        return pltpu.make_async_remote_copy(
            swap_out.at[owner], swap_in.at[owner], swap_send.at[owner], swap_recv.at[owner],
            device_id={"ctx": sibling}, device_id_type=MESH,
        )

    def pass_on(direction, owner, index, part):
        around = jnp.where(z == chips - 1, owner, z + 1)
        to = jnp.where(direction == 0, z - 1, around)
        return pltpu.make_async_remote_copy(
            ring_out.at[direction, index, part], ring_in.at[direction, index, part],
            r_send.at[direction, index, part], r_recv.at[direction, index, part],
            device_id={"ctx": 2 * to + core}, device_id_type=MESH,
        )

    @pl.loop(0, half + 1)
    def _(step):
        @pl.loop(0, 2)
        def _(direction):
            owner, valid = owed(direction, step)

            @pl.when(valid)
            def _():
                sums = keep.at[step % 2, direction]
                two(sums=sums, zo=owner)
                for part in range(2):
                    swap_out[owner, part] = sums[part, 1 - core].astype(swap_out.dtype)
                swap(owner).start()

        @pl.when(step >= 1)
        def _():
            before = step - 1

            @pl.loop(0, 2)
            def _(direction):
                owner, valid = owed(direction, before)

                @pl.when(valid)
                def _():
                    swap(owner).wait_recv()
                    arrives = jnp.logical_and(before >= 1, jnp.logical_or(direction == 1, z < chips - 1))
                    index = jnp.maximum(before - 1, 0)
                    for part in range(2):
                        here = keep.at[before % 2, direction, part, core]
                        here[...] += swap_in[owner, part].astype(F32)

                        @pl.when(arrives)
                        def _():
                            pass_on(direction, owner, index, part).wait_recv()
                            here[...] += ring_in[direction, index, part].astype(F32)

                        ring_out[direction, before, part] = here[...].astype(BF16)
                        pass_on(direction, owner, before, part).start()

    q_part = jnp.zeros((1, HD), F32)
    for h in range(heads):
        cols = slice(h * HD, (h + 1) * HD)
        x = q_raw[:, cols].astype(F32)
        upstream = scale * dq_t[:, cols].T
        grad, part = norm_back(x, inverse_rms(x), q_gain[...], upstream)
        q_part += part
        dq_out[:, cols] = grad.astype(BF16)
    store = pltpu.make_async_copy(dq_out, dq_hbm.at[0], store_sem)
    store.start()

    swap(z).wait_recv()
    for part in range(2):
        here = keep.at[half % 2, 0, part, core]
        here[...] += swap_in[z, part].astype(F32)

        @pl.when(z < chips - 1)
        def _():
            pass_on(0, z, half - 1, part).wait_recv()
            here[...] += ring_in[0, half - 1, part].astype(F32)

        @pl.when(z <= half - 2)
        def _():
            index = jnp.maximum(half - 2 - z, 0)
            pass_on(1, z, index, part).wait_recv()
            here[...] += ring_in[1, index, part].astype(F32)

    x = k_raw[...].astype(F32)
    upstream = scale * keep[half % 2, 0, 0, core]
    grad, k_part = norm_back(x, inverse_rms(x), k_gain[...], upstream)
    dk_out[0] = grad.astype(BF16)
    dv_out[0] = keep[half % 2, 0, 1, core].astype(BF16)

    def line_copy(i):
        to = (me + i) % n
        return pltpu.make_async_remote_copy(
            line_out, line_in.at[me], line_send.at[i], line_recv.at[me],
            device_id={"ctx": to}, device_id_type=MESH,
        )

    def line_arrival(i):
        source = (me + i) % n
        return pltpu.make_async_remote_copy(
            line_out, line_in.at[source], line_send.at[i], line_recv.at[source],
            device_id={"ctx": source}, device_id_type=MESH,
        )

    def plane_copy(i, slot):
        to = (place + i) % group
        return pltpu.make_async_remote_copy(
            plane_out, plane_in.at[slot], plane_send.at[i], plane_recv.at[slot],
            device_id={"tp": to // dp, "dp": to % dp}, device_id_type=MESH,
        )

    line_out[0:1] = q_part
    line_out[1:2] = k_part
    line_in[me] = line_out[...]

    @pl.loop(1, n)
    def _(i):
        line_copy(i).start()

    @pl.loop(1, n)
    def _(i):
        line_arrival(i).wait_recv()

    plane_out[...] = jnp.sum(line_in[...], axis=0)
    plane_in[place] = plane_out[...]

    @pl.loop(1, group)
    def _(i):
        plane_copy(i, place).start()

    @pl.loop(1, group)
    def _(i):
        plane_copy(i, (place + i) % group).wait_recv()

    gains_out[...] = jnp.sum(plane_in[...], axis=0)

    for part in range(2):
        @pl.when(first_up)
        def _():
            ring_copy(0, z, 0, part, z + 1).wait_send()

        @pl.when(first_around)
        def _():
            ring_copy(1, z, z, part, chips - 1).wait_send()

        sibling_copy(z, part, core).wait_send()

    @pl.loop(0, half)
    def _(step):
        @pl.loop(0, 2)
        def _(direction):
            owner, comes = gathered(direction, step)
            to, index, goes = forwarded(direction, step)

            @pl.when(comes)
            def _():
                for part in range(2):
                    @pl.when(goes)
                    def _():
                        ring_copy(direction, owner, index, part, to).wait_send()

                    sibling_copy(owner, part, core).wait_send()

            owner, valid = owed(direction, step)

            @pl.when(valid)
            def _():
                swap(owner).wait_send()
                for part in range(2):
                    pass_on(direction, owner, step, part).wait_send()

    swap(z).wait_send()

    @pl.loop(1, n)
    def _(i):
        line_copy(i).wait_send()

    @pl.loop(1, group)
    def _(i):
        plane_copy(i, place).wait_send()

    store.wait()


def solution(mesh):
    n, tp, dp = mesh.shape["ctx"], mesh.shape["tp"], mesh.shape["dp"]
    chips, half = n // 2, n // 4

    def shards(q_raw, k_raw, values_in, grad_out, q_gain, k_gain):
        rows, width = q_raw.shape[1:]
        flat = rows * width // HD
        whole = pl.BlockSpec(memory_space=pltpu.VMEM)
        anywhere = pl.BlockSpec(memory_space=pl.ANY)
        dma = pltpu.SemaphoreType.DMA
        outs = pl.pallas_call(
            functools.partial(kernel, n, tp, dp),
            out_shape=(
                jax.ShapeDtypeStruct(q_raw.shape, BF16),
                jax.ShapeDtypeStruct(k_raw.shape, BF16),
                jax.ShapeDtypeStruct(k_raw.shape, BF16),
                jax.ShapeDtypeStruct((2, HD), F32),
            ),
            in_specs=[anywhere] * 4 + [whole] * 2,
            out_specs=(anywhere, whole, whole, whole),
            scratch_shapes=[
                pltpu.VMEM((rows, width), BF16),
                pltpu.VMEM((rows, HD), BF16),
                pltpu.VMEM((flat, HD), BF16),
                pltpu.VMEM((flat, HD), BF16),
                pltpu.VMEM((n, 2, HD, HD), BF16),
                pltpu.VMEM((chips, 2 * HD, flat), F32),
                pltpu.VMEM((chips, 2 * HD, flat), F32),
                pltpu.VMEM((chips, 1, flat), F32),
                pltpu.VMEM((8, flat), F32),
                pltpu.VMEM((2 * HD, flat), BF16),
                pltpu.VMEM((2 * HD, flat), BF16),
                pltpu.VMEM((HD, flat), F32),
                pltpu.VMEM((rows, width), BF16),
                pltpu.VMEM((2, 2, 2, 2, HD, HD), F32),
                pltpu.VMEM((chips, 2, HD, HD), BF16),
                pltpu.VMEM((chips, 2, HD, HD), BF16),
                pltpu.VMEM((2, half, 2, HD, HD), BF16),
                pltpu.VMEM((2, half, 2, HD, HD), BF16),
                pltpu.VMEM((2, HD), F32),
                pltpu.VMEM((n, 2, HD), F32),
                pltpu.VMEM((2, HD), F32),
                pltpu.VMEM((tp * dp, 2, HD), F32),
                dma((3,)), dma((flat // HD,)), dma,
                dma((2, half, 2)), dma((2, half, 2)),
                dma((chips, 2)), dma((chips, 2)),
                dma((2, half, 2)), dma((2, half, 2)),
                dma((chips,)), dma((chips,)),
                dma((n,)), dma((n,)),
                dma((tp * dp,)), dma((tp * dp,)),
            ],
            compiler_params=pltpu.CompilerParams(
                collective_id=0, has_side_effects=True, vmem_limit_bytes=56 * 1024 * 1024
            ),
            cost_estimate=pl.CostEstimate(
                flops=10 * flat * n * rows * HD, bytes_accessed=6 * rows * width,
                transcendentals=flat * n * rows,
            ),
        )(q_raw, k_raw, values_in, grad_out, q_gain.reshape(1, HD), k_gain.reshape(1, HD))
        return outs

    spread = P("dp", "ctx", "tp")
    return jax.shard_map(
        shards,
        mesh=mesh,
        in_specs=(spread, spread, spread, spread, P(), P()),
        out_specs=(spread, spread, spread, P()),
        check_vma=False,
    )
```

time: 526 us -> 118 us (0.22)
  waiting for transfers between devices: 338 us -> 0 us
  Pallas kernels: 0 us -> 114 us
  blocking collectives: 106 us -> 0 us
  loops' own time: 25.5 us -> 0 us
  local copies, waits for them, and re-layouts: 22.4 us -> 3.68 us
  between operations: 14 us -> 0.65 us
  other arithmetic: 9.55 us -> 0 us
  matrix products: 8.35 us -> 0 us
    reduce_scatter x1 -> x0, waiting for transfers between devices: 194 us -> none  [shards(): lax.psum_scatter(key_tiles_out.reshape(total_keys, 2 * head_width), 'ctx'...]
    all_gather x2 -> x0, waiting for transfers between devices: 143 us -> none  [the longest x1 73.2 us: shards(): lax.all_gather(k_norm.reshape(row_count, head_width), 'ctx', axis=0, tile...]
    pallas_call x0 -> x1, Pallas kernels: none -> 114 us  [shards(): pl.pallas_call(functools.partial(kernel, n, tp, dp), out_shape=(jax.Shape...]
    psum x1 -> x0, blocking collectives: 106 us -> none  [shards(): q_total, k_total = lax.psum((q_part, k_part), ('ctx', 'tp', 'dp'))]
    another operation x18 -> x0, loops' own time: 25.5 us -> none  [the longest x1 10.6 us: shards(): lax.scan(first_pass, start_state, jnp.arange(num_blocks, dtype=jnp.int32))]
    dynamic_slice x16 -> x0, local copies, waits for them, and re-layouts: 9.37 us -> none  [shards(): lax.scan(first_pass, start_state, jnp.arange(num_blocks, dtype=jnp.int32))]
    dot_general x7 -> x0, matrix products: 8.35 us -> none  [the longest x2 3.02 us: score_block(): dprob = jnp.dot(cotans, vals_tile.T, preferred_element_type=jnp.float32)]
    dynamic_update_slice x16 -> x0, local copies, waits for them, and re-layouts: 8.33 us -> none  [shards(): lax.scan(second_pass, zero_queries, jnp.arange(num_blocks, dtype=jnp.int32))]
  transfers between devices with their start and end apart: 3 -> 0, of which waited for: 3 -> 0; matrix products, arithmetic and copies ran while one was open for 1% -> 0% of each run, Pallas kernels for 0% -> 0%
where the time goes in v1:
time: 118 us
  Pallas kernels  114 us (97%)
  local copies, waits for them, and re-layouts  3.68 us (3%)
    pallas_call x1, Pallas kernels, shards(): pl.pallas_call(functools.partial(kernel, n, tp, dp), out_shape=(jax.Shape...  114 us
    unnamed x10, local copies, waits for them, and re-layouts  3.68 us

profile of v1, /device:TPU:1, one launch (start us, length us, event | category | flops | bytes accessed | tf_op | source)
XLA Modules:
  0.0 117.9 jit_solution(17660401553168212814)
XLA Ops:
  0.6 113.6 %shard_map.93 = (bf16[1,128,1024]{2,1,0:T(8,128)(2,1)}, bf16[1,128,128]{2,1,0:T(8,128)(2,1)}, bf16[1,128,128]{2,1,0:T(8,128)(2,1)}, f32[2,128]{1,0:T(2,128)}) custom-call(bf16[1,128,1024]{2,1,0:T(8,128)(2,1)} %q_hbm.1, bf16[1,128,128]{2,1,0:T(8,128)(2,1)} %k_hbm.1, bf16[1,128,128]{2,1,0:T(8,128)(2,1)} %v_hbm.1, bf16[1,128,1024]{2,1,0:T(8,128)(2,1)} %g_hbm.1, ...), custom_call_target="tpu_custom_call" | custom-call | flops 5368709120 | bytes 786432 | tf_op jit(solution)/shard_map/pallas_call | solution.py:425
  114.2 0.0 copy-start.1
  114.2 1.7 %copy.14 = bf16[1,128,1024]{2,1,0:T(8,128)(2,1)} copy(bf16[1,128,1024]{2,1,0:T(8,128)(2,1)} %get-tuple-element.8) | data formatting | bytes 524288
  115.9 0.0 copy-done.1
  115.9 0.0 copy-start
  115.9 0.6 copy.15
  116.5 0.2 copy-done
  116.7 0.0 copy-start.2
  116.7 0.6 copy.16
  117.3 0.0 copy-done.2
  117.3 0.6 copy.17
Async XLA Ops:
  114.2 1.7 %copy-start.1 = (bf16[1,128,128]{2,1,0:T(8,128)(2,1)S(1)}, bf16[1,128,128]{2,1,0:T(8,128)(2,1)}, u32[]{:S(2)}) copy-start(bf16[1,128,128]{2,1,0:T(8,128)(2,1)} %get-tuple-element.9) | copy-start | bytes 98308
  115.9 0.8 copy-start
  116.7 0.7 copy-start.2

commit v2 on v1

v2 whole, which is shorter than its diff:
```python
import functools
import math

import jax
import jax.numpy as jnp
from jax import lax
from jax.experimental import pallas as pl
from jax.experimental.pallas import tpu as pltpu
from jax.sharding import PartitionSpec as P

HD = 128
CW = 256
EPS = 1e-06
MASKED = -1e30
F32 = jnp.float32
BF16 = jnp.bfloat16
MESH = pl.DeviceIdType.MESH

GATHER = {0: (1, 2), 2: (3, 4), 4: (5, 6), 6: (7, 8)}
SCATTER = {0: (1, 3), 1: (2,), 3: (4, 6), 4: (5,), 6: (7, 8)}
AROUND = {0: (1, 3), 1: (2,), 3: (4, 6), 4: (5,)}
WRAP = {0: (1, 3), 1: (2,), 3: (4, 5, 6)}
GATHER_ORDER = (2, 1, 4, 3, 6, 5, 8, 7)
SCATTER_ORDER = (8, 7, 5, 2, 6, 4, 1, 3)
AROUND_DELAY = {0: 1, 1: 3, 3: 3, 2: 5, 4: 5, 6: 5, 5: 6}
NEAR = 3


def pick(index, table):
    out = jnp.int32(-1)
    for key, value in table.items():
        out = jnp.where(index == key, value, out)
    return out


def children(tree, reach, slot):
    kept = {d: [c for c in cs if c <= reach] for d, cs in tree.items()}
    return {d: cs[slot] for d, cs in kept.items() if len(cs) > slot}


def height(place, owner, far):
    below = [1 + height(c, owner, far) for c in WRAP.get(place, ()) if owner <= far - c]
    return max(below, default=0)


def parents(tree, reach):
    return {c: d for d, cs in tree.items() for c in cs if c <= reach}


def dot(a, b, contract):
    return lax.dot_general(
        a, b, (((contract[0],), (contract[1],)), ((), ())), preferred_element_type=F32
    )


def inverse_rms(x):
    return lax.rsqrt(jnp.mean(x * x, axis=1, keepdims=True) + EPS)


def norm_back(x, inv, gain, upstream):
    scaled = gain * upstream
    inner = jnp.mean(scaled * x, axis=1, keepdims=True)
    grad = inv * scaled - x * (inv * inv * inv) * inner
    return grad, jnp.sum(upstream * x * inv, axis=0, keepdims=True)


def first_pass(kv, qh, go, probs, dprobs, block_max, stats, zo, core, diagonal, scale2):
    keys = kv[pl.ds(2 * zo, 2), 0].reshape(2 * HD, HD)
    vals = kv[pl.ds(2 * zo, 2), 1].reshape(2 * HD, HD)
    total = qh.shape[0]
    for start in range(0, total, CW):
        cols = slice(start, start + CW)
        s = dot(keys, qh[cols, :], (1, 1))
        if diagonal:
            key_pos = lax.broadcasted_iota(jnp.int32, (2 * HD, CW), 0)
            query_pos = core * HD + lax.broadcasted_iota(jnp.int32, (2 * HD, CW), 1) % HD
            s = jnp.where(key_pos <= query_pos, s, MASKED)
        dp = dot(vals, go[cols, :], (1, 1))
        top = jnp.max(s, axis=0, keepdims=True)
        if not diagonal:
            old = stats[0:1, cols]
            top = jnp.maximum(top, old)
        p = jnp.exp2(s * scale2 - top * scale2)
        mass = jnp.sum(p, axis=0, keepdims=True)
        weighted = jnp.sum(p * dp, axis=0, keepdims=True)
        if not diagonal:
            shrink = jnp.exp2((old - top) * scale2)
            mass += stats[1:2, cols] * shrink
            weighted += stats[2:3, cols] * shrink
        stats[0:1, cols] = top
        stats[1:2, cols] = mass
        stats[2:3, cols] = weighted
        block_max[zo, :, cols] = top
        probs[zo, :, cols] = p
        dprobs[zo, :, cols] = dp


def second_pass(kv, qh, go, probs, dprobs, block_max, stats, prob_b, dscore_b, dq_t, sums, zo, scale2):
    total = qh.shape[0]
    keys = kv[pl.ds(2 * zo, 2), 0].reshape(2 * HD, HD)
    for start in range(0, total, CW):
        cols = slice(start, start + CW)
        factor = jnp.exp2((block_max[zo, :, cols] - stats[0:1, cols]) * scale2) * stats[1:2, cols]
        p = probs[zo, :, cols] * factor
        ds = p * (dprobs[zo, :, cols] - stats[2:3, cols])
        prob_b[:, cols] = p.astype(BF16)
        ds = ds.astype(BF16)
        dscore_b[:, cols] = ds
        dq_t[:, cols] += dot(keys, ds, (0, 0))
    sums[0] = dot(dscore_b[...], qh[...], (1, 0)).reshape(2, HD, HD)
    sums[1] = dot(prob_b[...], go[...], (1, 0)).reshape(2, HD, HD)


def kernel(
    n, tp, dp,
    q_hbm, k_hbm, v_hbm, g_hbm, q_gain, k_gain,
    dq_hbm, dk_out, dv_out, gains_out,
    q_raw, k_raw, qh, go, kv, probs, dprobs, block_max, stats, prob_b, dscore_b, dq_t, dq_out,
    keep, swap_out, swap_in, down_out, down_in, wrap_out, wrap_in,
    pair_out, pair_in, line_out, line_in, plane_out, plane_in,
    load_sem, head_sem, store_sem, word,
    up_send, up_recv, around_send, around_recv, sib_send, sib_recv,
    down_send, down_recv, wrap_send, wrap_recv, swap_send, swap_recv,
    pair_send, pair_recv, line_send, line_recv, plane_send, plane_recv,
):
    chips, heads = n // 2, qh.shape[0] // HD
    reach = chips // 2
    far = chips - reach - 2
    top = chips - 1
    scale = HD ** (-0.5)
    scale2 = scale * math.log2(math.e)
    me = lax.axis_index("ctx")
    z, core = me // 2, me % 2
    sibling = me + 1 - 2 * core
    place = lax.axis_index("tp") * dp + lax.axis_index("dp")
    group = tp * dp
    below_top = top - z

    def chip(to):
        return {"ctx": 2 * to + core}

    def plane(to):
        return {"tp": to // dp, "dp": to % dp}

    barrier = pltpu.get_barrier_semaphore()

    def greet(to):
        pl.semaphore_signal(barrier, 1, device_id=chip(to), device_id_type=MESH)

    greeted = jnp.int32(group)
    for away in range(1, NEAR + 1):
        for to in (z + away, z - away):
            inside = jnp.logical_and(to >= 0, to <= top)
            greeted += jnp.where(inside, 1, 0)

            @pl.when(inside)
            def _():
                greet(to)

    greeted += jnp.where(z <= far, 1, 0)

    @pl.when(z == top)
    def _():
        @pl.loop(0, far + 1)
        def _(i):
            greet(i)

    pl.semaphore_signal(barrier, 1, device_id={"ctx": sibling}, device_id_type=MESH)

    @pl.loop(1, group)
    def _(i):
        pl.semaphore_signal(barrier, 1, device_id=plane((place + i) % group), device_id_type=MESH)

    def load(i):
        src, dst = ((k_hbm.at[0], k_raw), (v_hbm.at[0], kv.at[me, 1]), (q_hbm.at[0], q_raw))[i]
        return pltpu.make_async_copy(src, dst, load_sem.at[i])

    def load_head(h):
        return pltpu.make_async_copy(
            g_hbm.at[0, :, pl.ds(h * HD, HD)], go.at[pl.ds(h * HD, HD)], head_sem.at[h]
        )

    for i in range(3):
        load(i).start()
    for h in range(heads):
        load_head(h).start()

    load(0).wait()
    x = k_raw[...].astype(F32)
    kv[me, 0] = (x * inverse_rms(x) * k_gain[...]).astype(BF16)
    load(1).wait()

    def up_copy(owner, distance, part, to):
        block = kv.at[2 * owner + core, part]
        return pltpu.make_async_remote_copy(
            block, block, up_send.at[distance, part], up_recv.at[distance, part],
            device_id=chip(to), device_id_type=MESH,
        )

    def around_copy(owner, slot, part, to):
        block = kv.at[2 * owner + core, part]
        return pltpu.make_async_remote_copy(
            block, block, around_send.at[owner, slot, part], around_recv.at[owner, part],
            device_id=chip(to), device_id_type=MESH,
        )

    def sibling_copy(owner, owner_core):
        block = kv.at[2 * owner + owner_core]
        return pltpu.make_async_remote_copy(
            block, block, sib_send.at[owner], sib_recv.at[owner],
            device_id={"ctx": sibling}, device_id_type=MESH,
        )

    def each_up_send(distance, part, act):
        for slot in (1, 0):
            child = pick(distance, children(GATHER, reach, slot))
            to = z + child - distance

            @pl.when(jnp.logical_and(child > 0, to <= top))
            def _():
                act(up_copy(z - distance, child, part, to))

    def each_around_send(owner, part, act):
        for slot in (1, 0):
            child = pick(below_top, children(AROUND, far, slot))

            @pl.when(jnp.logical_and(child > 0, owner <= far - child))
            def _():
                act(around_copy(owner, slot, part, top - child))

    def each_own_send(act):
        for part in range(2):
            @pl.when(z <= far)
            def _():
                act(around_copy(z, 0, part, top))

            each_up_send(0, part, act)

        act(sibling_copy(z, core))

    pl.semaphore_wait(barrier, greeted)
    each_own_send(lambda copy: copy.start())

    load(2).wait()
    for h in range(heads):
        cols = slice(h * HD, (h + 1) * HD)
        x = q_raw[:, cols].astype(F32)
        qh[cols, :] = (x * inverse_rms(x) * q_gain[...]).astype(BF16)
    for h in range(heads):
        load_head(h).wait()

    one = functools.partial(
        first_pass, kv, qh, go, probs, dprobs, block_max, stats, core=core, scale2=scale2
    )
    two = functools.partial(
        second_pass, kv, qh, go, probs, dprobs, block_max, stats, prob_b, dscore_b, dq_t, scale2=scale2
    )

    sibling_copy(z, 1 - core).wait_recv()
    one(zo=z, diagonal=True)

    up_table = {i: d for i, d in enumerate(d for d in GATHER_ORDER if d <= reach)}
    delay = pick(below_top, AROUND_DELAY)
    gather_steps = max(reach, 1 + max((far - d) // 2 + late for d, late in AROUND_DELAY.items() if d <= far))
    word_step = jnp.minimum(2 * (below_top // NEAR), gather_steps)

    def gathered(source, step):
        distance = pick(step, up_table)
        up = z - distance
        around = 2 * (step - delay) + source - 1
        up_valid = jnp.logical_and(distance > 0, up >= 0)
        around_valid = jnp.logical_and(
            below_top <= far, jnp.logical_and(step >= delay, around <= far - below_top)
        )
        owner = jnp.where(source == 0, up, around)
        return owner, jnp.logical_or(
            jnp.logical_and(source == 0, up_valid), jnp.logical_and(source >= 1, around_valid)
        )

    def each_passed_on(source, step, arrival, act):
        owner, comes = gathered(source, step)

        @pl.when(jnp.logical_and(comes, source == 0))
        def _():
            for part in range(2):
                if arrival:
                    up_copy(owner, z - owner, part, z).wait_recv()
                each_up_send(z - owner, part, act)

        @pl.when(jnp.logical_and(comes, source >= 1))
        def _():
            for part in range(2):
                if arrival:
                    around_copy(owner, 0, part, z).wait_recv()
                each_around_send(owner, part, act)

        @pl.when(comes)
        def _():
            act(sibling_copy(owner, core))

    @pl.loop(0, gather_steps + 1)
    def _(step):
        @pl.when(step == word_step)
        def _():
            @pl.when(z + NEAR <= top)
            def _():
                pl.semaphore_wait(word, 1)

            @pl.when(z >= NEAR)
            def _():
                pl.semaphore_signal(word, 1, device_id=chip(z - NEAR), device_id_type=MESH)

        @pl.loop(0, 3)
        def _(source):
            each_passed_on(source, step, True, lambda copy: copy.start())
            owner, comes = gathered(source, step - 1)

            @pl.when(comes)
            def _():
                sibling_copy(owner, 1 - core).wait_recv()
                one(zo=owner, diagonal=False)

    inv_mass = 1.0 / stats[1:2, :]
    stats[2:3, :] = stats[2:3, :] * inv_mass
    stats[1:2, :] = inv_mass
    dq_t[...] = jnp.zeros_like(dq_t)

    order = [d for d in SCATTER_ORDER if d <= reach]
    down_table = {i: d for i, d in enumerate(order)}
    down_table[reach] = 0
    down_parent, wrap_parent = parents(SCATTER, reach), parents(WRAP, far)
    wrap_slot = {c: i for cs in WRAP.values() for i, c in enumerate(cs)}

    def owed(direction, step):
        distance = pick(step, down_table)
        down = z - distance
        around = z - reach - 1 - step
        owner = jnp.where(direction == 0, down, around)
        limit = jnp.where(direction == 0, distance >= 0, jnp.logical_and(step >= 0, step <= far))
        return owner, jnp.logical_and(owner >= 0, limit)

    def swap(owner):
        return pltpu.make_async_remote_copy(
            swap_out.at[owner], swap_in.at[owner], swap_send.at[owner], swap_recv.at[owner],
            device_id={"ctx": sibling}, device_id_type=MESH,
        )

    def down_copy(distance, part, to):
        return pltpu.make_async_remote_copy(
            down_out.at[distance, part], down_in.at[distance, part],
            down_send.at[distance, part], down_recv.at[distance, part],
            device_id=chip(to), device_id_type=MESH,
        )

    def wrap_copy(owner, slot, part, to):
        return pltpu.make_async_remote_copy(
            wrap_out.at[owner, part], wrap_in.at[owner, slot, part],
            wrap_send.at[owner, part], wrap_recv.at[owner, slot, part],
            device_id=chip(to), device_id_type=MESH,
        )

    def add_swapped(step, direction, owner):
        swap(owner).wait_recv()
        for part in range(2):
            keep[step, direction, part, core] += swap_in[owner, part].astype(F32)

    def add_down(step, distance, part):
        for slot in range(2):
            child = pick(distance, children(SCATTER, reach, slot))

            @pl.when(jnp.logical_and(child > 0, z + child - distance <= top))
            def _():
                down_copy(child, part, z).wait_recv()
                keep[step, 0, part, core] += down_in[child, part].astype(F32)

    def add_wrap(step, owner, part):
        for slot in range(3):
            child = pick(below_top, children(WRAP, far, slot))

            @pl.when(jnp.logical_and(child > 0, owner <= far - child))
            def _():
                wrap_copy(owner, slot, part, z).wait_recv()
                keep[step, 1, part, core] += wrap_in[owner, slot, part].astype(F32)

    def down_target(distance):
        return z - distance + pick(distance, down_parent)

    def each_wrap_send(owner, part, act):
        for slot in range(3):
            @pl.when(pick(below_top, wrap_slot) == slot)
            def _():
                act(wrap_copy(owner, slot, part, top - pick(below_top, wrap_parent)))

        @pl.when(below_top == 0)
        def _():
            act(wrap_copy(owner, 0, part, owner))

    def finish_down(step):
        owner, valid = owed(0, step)

        @pl.when(valid)
        def _():
            distance = z - owner
            add_swapped(step, 0, owner)
            for part in range(2):
                add_down(step, distance, part)
                down_out[distance, part] = keep[step, 0, part, core].astype(BF16)
                down_copy(distance, part, down_target(distance)).start()

    heights = {(p, e): height(p, e, far) for p in range(far + 1) for e in range(far - p + 1)}
    tallest = max(heights.values())

    def finish_wrap(now):
        step = jnp.int32(-1)
        for tall in range(tallest + 1):
            before = now - 1 - 2 * tall
            owner, valid = owed(1, before)
            keys = {p * chips + e: tall for (p, e), h in heights.items() if h == tall}
            due = jnp.logical_and(valid, pick(below_top * chips + owner, keys) == tall)
            step = jnp.where(due, before, step)
        owner, valid = owed(1, step)

        @pl.when(valid)
        def _():
            add_swapped(step, 1, owner)
            for part in range(2):
                add_wrap(step, owner, part)
                wrap_out[owner, part] = keep[step, 1, part, core].astype(BF16)
                each_wrap_send(owner, part, lambda copy: copy.start())

    @pl.loop(0, reach + 1)
    def _(step):
        @pl.loop(0, 2)
        def _(direction):
            owner, valid = owed(direction, step)

            @pl.when(valid)
            def _():
                sums = keep.at[step, direction]
                two(sums=sums, zo=owner)
                for part in range(2):
                    swap_out[owner, part] = sums[part, 1 - core].astype(BF16)
                swap(owner).start()

            @pl.when(direction == 0)
            def _():
                finish_wrap(step)

            @pl.when(direction == 1)
            def _():
                finish_down(step - 1)

    q_part = jnp.zeros((1, HD), F32)
    for h in range(heads):
        cols = slice(h * HD, (h + 1) * HD)
        x = q_raw[:, cols].astype(F32)
        upstream = scale * dq_t[:, cols].T
        grad, part = norm_back(x, inverse_rms(x), q_gain[...], upstream)
        q_part += part
        dq_out[:, cols] = grad.astype(BF16)
    store = pltpu.make_async_copy(dq_out, dq_hbm.at[0], store_sem)
    store.start()

    pair = pltpu.make_async_remote_copy(
        pair_out, pair_in, pair_send, pair_recv, device_id={"ctx": sibling}, device_id_type=MESH
    )

    def offset(i, count):
        away = (i + 1) // 2
        return count // 2 + jnp.where(i % 2 == 1, -away, away)

    def line_copy(i, slot):
        away = offset(i, chips)
        return pltpu.make_async_remote_copy(
            line_out, line_in.at[slot], line_send.at[i], line_recv.at[slot],
            device_id=chip((z + away) % chips), device_id_type=MESH,
        )

    def plane_copy(i, slot):
        return pltpu.make_async_remote_copy(
            plane_out, plane_in.at[slot], plane_send.at[i], plane_recv.at[slot],
            device_id=plane((place + i + 1) % group), device_id_type=MESH,
        )

    pair_out[...] = q_part
    pair.start()

    @pl.loop(reach + 1, far + 2 + 2 * tallest)
    def _(step):
        finish_wrap(step)

    pair.wait_recv()
    line_out[...] = pair_out[...] + pair_in[...]
    line_in[z] = line_out[...]

    @pl.loop(0, chips - 1)
    def _(i):
        line_copy(i, z).start()

    add_swapped(reach, 0, z)
    for part in range(2):
        add_down(reach, 0, part)

    @pl.when(z <= far)
    def _():
        for part in range(2):
            wrap_copy(z, 0, part, z).wait_recv()
            keep[reach, 0, part, core] += wrap_in[z, 0, part].astype(F32)

    x = k_raw[...].astype(F32)
    upstream = scale * keep[reach, 0, 0, core]
    grad, _ = norm_back(x, inverse_rms(x), k_gain[...], upstream)
    dk_out[0] = grad.astype(BF16)
    dv_out[0] = keep[reach, 0, 1, core].astype(BF16)

    @pl.loop(0, chips - 1)
    def _(i):
        line_copy(i, (z + offset(i, chips)) % chips).wait_recv()

    plane_out[...] = jnp.sum(line_in[...], axis=0)
    plane_in[place] = plane_out[...]

    @pl.loop(0, group - 1)
    def _(i):
        plane_copy(i, place).start()

    @pl.loop(0, group - 1)
    def _(i):
        plane_copy(i, (place + i + 1) % group).wait_recv()

    q_total = jnp.sum(plane_in[...], axis=0)
    gains_out[0:1] = q_total
    gains_out[1:2] = q_total * q_gain[...] / k_gain[...]

    def left(copy):
        copy.wait_send()

    each_own_send(left)

    @pl.loop(0, gather_steps)
    def _(step):
        @pl.loop(0, 3)
        def _(source):
            each_passed_on(source, step, False, left)

    @pl.loop(0, reach + 1)
    def _(step):
        owner, valid = owed(0, step)

        @pl.when(valid)
        def _():
            swap(owner).wait_send()

            @pl.when(owner < z)
            def _():
                for part in range(2):
                    down_copy(z - owner, part, down_target(z - owner)).wait_send()

        around, around_valid = owed(1, step)

        @pl.when(around_valid)
        def _():
            swap(around).wait_send()
            for part in range(2):
                each_wrap_send(around, part, left)

    pair.wait_send()

    @pl.loop(0, chips - 1)
    def _(i):
        line_copy(i, z).wait_send()

    @pl.loop(0, group - 1)
    def _(i):
        plane_copy(i, place).wait_send()

    store.wait()


def solution(mesh):
    n, tp, dp = mesh.shape["ctx"], mesh.shape["tp"], mesh.shape["dp"]
    chips, reach = n // 2, n // 4
    far = chips - reach - 2

    def shards(q_raw, k_raw, values_in, grad_out, q_gain, k_gain):
        rows, width = q_raw.shape[1:]
        flat = rows * width // HD
        whole = pl.BlockSpec(memory_space=pltpu.VMEM)
        anywhere = pl.BlockSpec(memory_space=pl.ANY)
        dma = pltpu.SemaphoreType.DMA
        outs = pl.pallas_call(
            functools.partial(kernel, n, tp, dp),
            out_shape=(
                jax.ShapeDtypeStruct(q_raw.shape, BF16),
                jax.ShapeDtypeStruct(k_raw.shape, BF16),
                jax.ShapeDtypeStruct(k_raw.shape, BF16),
                jax.ShapeDtypeStruct((2, HD), F32),
            ),
            in_specs=[anywhere] * 4 + [whole] * 2,
            out_specs=(anywhere, whole, whole, whole),
            scratch_shapes=[
                pltpu.VMEM((rows, width), BF16),
                pltpu.VMEM((rows, HD), BF16),
                pltpu.VMEM((flat, HD), BF16),
                pltpu.VMEM((flat, HD), BF16),
                pltpu.VMEM((n, 2, HD, HD), BF16),
                pltpu.VMEM((chips, 2 * HD, flat), F32),
                pltpu.VMEM((chips, 2 * HD, flat), F32),
                pltpu.VMEM((chips, 1, flat), F32),
                pltpu.VMEM((8, flat), F32),
                pltpu.VMEM((2 * HD, flat), BF16),
                pltpu.VMEM((2 * HD, flat), BF16),
                pltpu.VMEM((HD, flat), F32),
                pltpu.VMEM((rows, width), BF16),
                pltpu.VMEM((reach + 1, 2, 2, 2, HD, HD), F32),
                pltpu.VMEM((chips, 2, HD, HD), BF16),
                pltpu.VMEM((chips, 2, HD, HD), BF16),
                pltpu.VMEM((reach + 1, 2, HD, HD), BF16),
                pltpu.VMEM((reach + 1, 2, HD, HD), BF16),
                pltpu.VMEM((far + 1, 2, HD, HD), BF16),
                pltpu.VMEM((far + 1, 3, 2, HD, HD), BF16),
                pltpu.VMEM((1, HD), F32),
                pltpu.VMEM((1, HD), F32),
                pltpu.VMEM((1, HD), F32),
                pltpu.VMEM((chips, 1, HD), F32),
                pltpu.VMEM((1, HD), F32),
                pltpu.VMEM((tp * dp, 1, HD), F32),
                dma((3,)), dma((flat // HD,)), dma, pltpu.SemaphoreType.REGULAR,
                dma((reach + 1, 2)), dma((reach + 1, 2)),
                dma((far + 1, 2, 2)), dma((far + 1, 2)),
                dma((chips,)), dma((chips,)),
                dma((reach + 1, 2)), dma((reach + 1, 2)),
                dma((far + 1, 2)), dma((far + 1, 3, 2)),
                dma((chips,)), dma((chips,)),
                dma, dma, dma((chips,)), dma((chips,)),
                dma((tp * dp,)), dma((tp * dp,)),
            ],
            compiler_params=pltpu.CompilerParams(
                collective_id=0, has_side_effects=True, vmem_limit_bytes=60 * 1024 * 1024
            ),
            cost_estimate=pl.CostEstimate(
                flops=10 * flat * n * rows * HD, bytes_accessed=6 * rows * width,
                transcendentals=flat * n * rows,
            ),
        )(q_raw, k_raw, values_in, grad_out, q_gain.reshape(1, HD), k_gain.reshape(1, HD))
        return outs

    spread = P("dp", "ctx", "tp")
    return jax.shard_map(
        shards,
        mesh=mesh,
        in_specs=(spread, spread, spread, spread, P(), P()),
        out_specs=(spread, spread, spread, P()),
        check_vma=False,
    )
```

time: 118 us -> 84.9 us (0.72)
  Pallas kernels: 114 us -> 80.3 us
    pallas_call x1, Pallas kernels: 114 us -> 80.3 us  [shards(): pl.pallas_call(functools.partial(kernel, n, tp, dp), out_shape=(jax.Shape...]
where the time goes in v2:
time: 84.9 us; the launch traced here: 84.6 us
  Pallas kernels  80.3 us (95%)
  local copies, waits for them, and re-layouts  3.68 us (4%)
    pallas_call x1, Pallas kernels, shards(): pl.pallas_call(functools.partial(kernel, n, tp, dp), out_shape=(jax.Shape...  80.3 us
    unnamed x10, local copies, waits for them, and re-layouts  3.68 us

profile of v2, /device:TPU:1, one launch (start us, length us, event | category | flops | bytes accessed | tf_op | source)
XLA Modules:
  0.0 84.6 jit_solution(5745271267082800147)
XLA Ops:
  0.6 80.3 %shard_map.93 = (bf16[1,128,1024]{2,1,0:T(8,128)(2,1)}, bf16[1,128,128]{2,1,0:T(8,128)(2,1)}, bf16[1,128,128]{2,1,0:T(8,128)(2,1)}, f32[2,128]{1,0:T(2,128)}) custom-call(bf16[1,128,1024]{2,1,0:T(8,128)(2,1)} %q_hbm.1, bf16[1,128,128]{2,1,0:T(8,128)(2,1)} %k_hbm.1, bf16[1,128,128]{2,1,0:T(8,128)(2,1)} %v_hbm.1, bf16[1,128,1024]{2,1,0:T(8,128)(2,1)} %g_hbm.1, ...), custom_call_target="tpu_custom_call" | custom-call | flops 5368709120 | bytes 786432 | tf_op jit(solution)/shard_map/pallas_call | solution.py:591
  80.9 0.0 copy-start.1
  80.9 1.7 %copy.14 = bf16[1,128,1024]{2,1,0:T(8,128)(2,1)} copy(bf16[1,128,1024]{2,1,0:T(8,128)(2,1)} %get-tuple-element.8) | data formatting | bytes 524288
  82.6 0.0 copy-done.1
  82.6 0.0 copy-start
  82.6 0.6 copy.15
  83.2 0.2 copy-done
  83.4 0.0 copy-start.2
  83.4 0.6 copy.16
  84.0 0.0 copy-done.2
  84.0 0.6 copy.17
Async XLA Ops:
  80.9 1.7 %copy-start.1 = (bf16[1,128,128]{2,1,0:T(8,128)(2,1)S(1)}, bf16[1,128,128]{2,1,0:T(8,128)(2,1)}, u32[]{:S(2)}) copy-start(bf16[1,128,128]{2,1,0:T(8,128)(2,1)} %get-tuple-element.9) | copy-start | bytes 98308
  82.6 0.8 copy-start
  83.4 0.7 copy-start.2

commit v3 on v2

--- a/solution.py
+++ b/solution.py
@@ -16,13 +16,15 @@
 BF16 = jnp.bfloat16
 MESH = pl.DeviceIdType.MESH
 
-GATHER = {0: (1, 2), 2: (3, 4), 4: (5, 6), 6: (7, 8)}
+GATHER = {0: (1, 3), 1: (2,), 3: (4, 6), 4: (5,), 6: (7, 8)}
 SCATTER = {0: (1, 3), 1: (2,), 3: (4, 6), 4: (5,), 6: (7, 8)}
 AROUND = {0: (1, 3), 1: (2,), 3: (4, 6), 4: (5,)}
 WRAP = {0: (1, 3), 1: (2,), 3: (4, 5, 6)}
-GATHER_ORDER = (2, 1, 4, 3, 6, 5, 8, 7)
+GATHER_ORDER = (1, 3, 2, 4, 6, 5, 7, 8)
 SCATTER_ORDER = (8, 7, 5, 2, 6, 4, 1, 3)
-AROUND_DELAY = {0: 1, 1: 3, 3: 3, 2: 5, 4: 5, 6: 5, 5: 6}
+AROUND_DELAY = {0: 0, 1: 2, 3: 2, 2: 4, 4: 4, 6: 4, 5: 5}
+WRAP_UP = False
+WRAP_LAG = (1, 2)
 NEAR = 3
 
 
@@ -117,11 +119,11 @@
     dq_hbm, dk_out, dv_out, gains_out,
     q_raw, k_raw, qh, go, kv, probs, dprobs, block_max, stats, prob_b, dscore_b, dq_t, dq_out,
     keep, swap_out, swap_in, down_out, down_in, wrap_out, wrap_in,
-    pair_out, pair_in, line_out, line_in, plane_out, plane_in,
+    line_out, line_in, plane_out, plane_in,
     load_sem, head_sem, store_sem, word,
     up_send, up_recv, around_send, around_recv, sib_send, sib_recv,
     down_send, down_recv, wrap_send, wrap_recv, swap_send, swap_recv,
-    pair_send, pair_recv, line_send, line_recv, plane_send, plane_recv,
+    line_send, line_recv, plane_send, plane_recv,
 ):
     chips, heads = n // 2, qh.shape[0] // HD
     reach = chips // 2
@@ -334,9 +336,9 @@
     def owed(direction, step):
         distance = pick(step, down_table)
         down = z - distance
-        around = z - reach - 1 - step
+        around = step if WRAP_UP else z - reach - 1 - step
         owner = jnp.where(direction == 0, down, around)
-        limit = jnp.where(direction == 0, distance >= 0, jnp.logical_and(step >= 0, step <= far))
+        limit = jnp.where(direction == 0, distance >= 0, jnp.logical_and(step >= 0, step < z - reach))
         return owner, jnp.logical_and(owner >= 0, limit)
 
     def swap(owner):
@@ -407,26 +409,22 @@
                 down_out[distance, part] = keep[step, 0, part, core].astype(BF16)
                 down_copy(distance, part, down_target(distance)).start()
 
-    heights = {(p, e): height(p, e, far) for p in range(far + 1) for e in range(far - p + 1)}
+    heights = {p * chips + e: height(p, e, far) for p in range(far + 1) for e in range(far - p + 1)}
     tallest = max(heights.values())
 
     def finish_wrap(now):
-        step = jnp.int32(-1)
-        for tall in range(tallest + 1):
-            before = now - 1 - 2 * tall
-            owner, valid = owed(1, before)
-            keys = {p * chips + e: tall for (p, e), h in heights.items() if h == tall}
-            due = jnp.logical_and(valid, pick(below_top * chips + owner, keys) == tall)
-            step = jnp.where(due, before, step)
-        owner, valid = owed(1, step)
-
-        @pl.when(valid)
-        def _():
-            add_swapped(step, 1, owner)
-            for part in range(2):
-                add_wrap(step, owner, part)
-                wrap_out[owner, part] = keep[step, 1, part, core].astype(BF16)
-                each_wrap_send(owner, part, lambda copy: copy.start())
+        @pl.loop(0, tallest + 1)
+        def _(tall):
+            step = now - WRAP_LAG[0] - WRAP_LAG[1] * tall
+            owner, valid = owed(1, step)
+
+            @pl.when(jnp.logical_and(valid, pick(below_top * chips + owner, heights) == tall))
+            def _():
+                add_swapped(step, 1, owner)
+                for part in range(2):
+                    add_wrap(step, owner, part)
+                    wrap_out[owner, part] = keep[step, 1, part, core].astype(BF16)
+                    each_wrap_send(owner, part, lambda copy: copy.start())
 
     @pl.loop(0, reach + 1)
     def _(step):
@@ -461,41 +459,43 @@
     store = pltpu.make_async_copy(dq_out, dq_hbm.at[0], store_sem)
     store.start()
 
-    pair = pltpu.make_async_remote_copy(
-        pair_out, pair_in, pair_send, pair_recv, device_id={"ctx": sibling}, device_id_type=MESH
-    )
-
     def offset(i, count):
         away = (i + 1) // 2
         return count // 2 + jnp.where(i % 2 == 1, -away, away)
 
     def line_copy(i, slot):
-        away = offset(i, chips)
         return pltpu.make_async_remote_copy(
             line_out, line_in.at[slot], line_send.at[i], line_recv.at[slot],
-            device_id=chip((z + away) % chips), device_id_type=MESH,
+            device_id={"ctx": (me + offset(i, n)) % n}, device_id_type=MESH,
         )
 
     def plane_copy(i, slot):
         return pltpu.make_async_remote_copy(
             plane_out, plane_in.at[slot], plane_send.at[i], plane_recv.at[slot],
-            device_id=plane((place + i + 1) % group), device_id_type=MESH,
-        )
-
-    pair_out[...] = q_part
-    pair.start()
-
-    @pl.loop(reach + 1, far + 2 + 2 * tallest)
+            device_id=plane((place + offset(i, group)) % group), device_id_type=MESH,
+        )
+
+    line_out[...] = q_part
+    line_in[me] = q_part
+
+    @pl.loop(0, n - 1)
+    def _(i):
+        line_copy(i, me).start()
+
+    @pl.loop(reach + 1, far + 1 + WRAP_LAG[0] + WRAP_LAG[1] * tallest)
     def _(step):
         finish_wrap(step)
 
-    pair.wait_recv()
-    line_out[...] = pair_out[...] + pair_in[...]
-    line_in[z] = line_out[...]
-
-    @pl.loop(0, chips - 1)
+    @pl.loop(0, n - 1)
     def _(i):
-        line_copy(i, z).start()
+        line_copy(i, (me + offset(i, n)) % n).wait_recv()
+
+    plane_out[...] = jnp.sum(line_in[...], axis=0)
+    plane_in[place] = plane_out[...]
+
+    @pl.loop(0, group - 1)
+    def _(i):
+        plane_copy(i, place).start()
 
     add_swapped(reach, 0, z)
     for part in range(2):
@@ -513,20 +513,9 @@
     dk_out[0] = grad.astype(BF16)
     dv_out[0] = keep[reach, 0, 1, core].astype(BF16)
 
-    @pl.loop(0, chips - 1)
-    def _(i):
-        line_copy(i, (z + offset(i, chips)) % chips).wait_recv()
-
-    plane_out[...] = jnp.sum(line_in[...], axis=0)
-    plane_in[place] = plane_out[...]
-
     @pl.loop(0, group - 1)
     def _(i):
-        plane_copy(i, place).start()
-
-    @pl.loop(0, group - 1)
-    def _(i):
-        plane_copy(i, (place + i + 1) % group).wait_recv()
+        plane_copy(i, (place + offset(i, group)) % group).wait_recv()
 
     q_total = jnp.sum(plane_in[...], axis=0)
     gains_out[0:1] = q_total
@@ -564,17 +553,21 @@
             for part in range(2):
                 each_wrap_send(around, part, left)
 
-    pair.wait_send()
-
-    @pl.loop(0, chips - 1)
+    @pl.loop(0, n - 1)
     def _(i):
-        line_copy(i, z).wait_send()
+        line_copy(i, me).wait_send()
 
     @pl.loop(0, group - 1)
     def _(i):
         plane_copy(i, place).wait_send()
 
     store.wait()
+
+
+def hand_over(*refs):
+    count = len(refs) // 2
+    for i in range(count):
+        refs[count + i][...] = refs[i][...]
 
 
 def solution(mesh):
@@ -620,9 +613,7 @@
                 pltpu.VMEM((far + 1, 2, HD, HD), BF16),
                 pltpu.VMEM((far + 1, 3, 2, HD, HD), BF16),
                 pltpu.VMEM((1, HD), F32),
-                pltpu.VMEM((1, HD), F32),
-                pltpu.VMEM((1, HD), F32),
-                pltpu.VMEM((chips, 1, HD), F32),
+                pltpu.VMEM((n, 1, HD), F32),
                 pltpu.VMEM((1, HD), F32),
                 pltpu.VMEM((tp * dp, 1, HD), F32),
                 dma((3,)), dma((flat // HD,)), dma, pltpu.SemaphoreType.REGULAR,
@@ -632,7 +623,7 @@
                 dma((reach + 1, 2)), dma((reach + 1, 2)),
                 dma((far + 1, 2)), dma((far + 1, 3, 2)),
                 dma((chips,)), dma((chips,)),
-                dma, dma, dma((chips,)), dma((chips,)),
+                dma((n,)), dma((n,)),
                 dma((tp * dp,)), dma((tp * dp,)),
             ],
             compiler_params=pltpu.CompilerParams(
@@ -643,7 +634,12 @@
                 transcendentals=flat * n * rows,
             ),
         )(q_raw, k_raw, values_in, grad_out, q_gain.reshape(1, HD), k_gain.reshape(1, HD))
-        return outs
+        return pl.pallas_call(
+            hand_over,
+            out_shape=tuple(jax.ShapeDtypeStruct(x.shape, x.dtype) for x in outs),
+            in_specs=[whole] * len(outs),
+            out_specs=(whole,) * len(outs),
+        )(*outs)
 
     spread = P("dp", "ctx", "tp")
     return jax.shard_map(

time: 84.9 us -> 83.5 us (0.984)
  local copies, waits for them, and re-layouts: 3.68 us -> 0 us
  Pallas kernels: 80.3 us -> 82.7 us
    unnamed x10 -> x0, local copies, waits for them, and re-layouts: 3.68 us -> none
    pallas_call x0 -> x1, Pallas kernels: none -> 1.7 us  [shards(): pl.pallas_call(hand_over, out_shape=tuple((jax.ShapeDtypeStruct(x.shape,...]
where the time goes in v3:
time: 83.5 us; the launch traced here: 83.3 us
  Pallas kernels  82.7 us (99%)
    pallas_call x1, Pallas kernels, shards(): pl.pallas_call(functools.partial(kernel, n, tp, dp), out_shape=(jax.Shape...  81 us
    pallas_call x1, Pallas kernels, shards(): pl.pallas_call(hand_over, out_shape=tuple((jax.ShapeDtypeStruct(x.shape,...  1.7 us

profile of v3, /device:TPU:1, one launch (start us, length us, event | category | flops | bytes accessed | tf_op | source)
XLA Modules:
  0.0 83.3 jit_solution(2573452826046887629)
XLA Ops:
  0.6 81.0 %shard_map.93 = (bf16[1,128,1024]{2,1,0:T(8,128)(2,1)}, bf16[1,128,128]{2,1,0:T(8,128)(2,1)}, bf16[1,128,128]{2,1,0:T(8,128)(2,1)}, f32[2,128]{1,0:T(2,128)}) custom-call(bf16[1,128,1024]{2,1,0:T(8,128)(2,1)} %q_hbm.1, bf16[1,128,128]{2,1,0:T(8,128)(2,1)} %k_hbm.1, bf16[1,128,128]{2,1,0:T(8,128)(2,1)} %v_hbm.1, bf16[1,128,1024]{2,1,0:T(8,128)(2,1)} %g_hbm.1, ...), custom_call_target="tpu_custom_call" | custom-call | flops 5368709120 | bytes 786432 | tf_op jit(solution)/shard_map/pallas_call | solution.py:584
  81.6 1.7 %shard_map.94 = (bf16[1,128,1024]{2,1,0:T(8,128)(2,1)}, bf16[1,128,128]{2,1,0:T(8,128)(2,1)}, bf16[1,128,128]{2,1,0:T(8,128)(2,1)}, f32[2,128]{1,0:T(2,128)}) custom-call(bf16[1,128,1024]{2,1,0:T(8,128)(2,1)} %get-tuple-element.8.refs_0_, bf16[1,128,128]{2,1,0:T(8,128)(2,1)} %get-tuple-element.9.refs_1_, bf16[1,128,128]{2,1,0:T(8,128)(2,1)} %get-tuple-element.10.refs_2_, ...), custom_call_target="tpu_custom_call" | custom-call | tf_op jit(solution)/shard_map/pallas_call | solution.py:637

commit v4 on v3

--- a/solution.py
+++ b/solution.py
@@ -397,17 +397,31 @@
         def _():
             act(wrap_copy(owner, 0, part, owner))
 
-    def finish_down(step):
+    def waits_down(distance):
+        out = False
+        for slot in range(2):
+            child = pick(distance, children(SCATTER, reach, slot))
+            out = jnp.logical_or(out, jnp.logical_and(child > 0, z + child - distance <= top))
+        return out
+
+    def finish_down(step, waiting):
         owner, valid = owed(0, step)
+        valid = jnp.logical_and(valid, waits_down(z - owner) == waiting)
 
         @pl.when(valid)
         def _():
             distance = z - owner
-            add_swapped(step, 0, owner)
+            to = down_target(distance)
+            swap(owner).wait_recv()
             for part in range(2):
-                add_down(step, distance, part)
-                down_out[distance, part] = keep[step, 0, part, core].astype(BF16)
-                down_copy(distance, part, down_target(distance)).start()
+                if waiting:
+                    keep[step, 0, part, core] += swap_in[owner, part].astype(F32)
+                    add_down(step, distance, part)
+                    down_out[distance, part] = keep[step, 0, part, core].astype(BF16)
+                else:
+                    both = keep[step, 0, part, core] + swap_in[owner, part].astype(F32)
+                    down_out[distance, part] = both.astype(BF16)
+                down_copy(distance, part, to).start()
 
     heights = {p * chips + e: height(p, e, far) for p in range(far + 1) for e in range(far - p + 1)}
     tallest = max(heights.values())
@@ -446,7 +460,7 @@
 
             @pl.when(direction == 1)
             def _():
-                finish_down(step - 1)
+                finish_down(step - 1, False)
 
     q_part = jnp.zeros((1, HD), F32)
     for h in range(heads):
@@ -482,9 +496,16 @@
     def _(i):
         line_copy(i, me).start()
 
-    @pl.loop(reach + 1, far + 1 + WRAP_LAG[0] + WRAP_LAG[1] * tallest)
+    last = far + 1 + WRAP_LAG[0] + WRAP_LAG[1] * tallest
+    @pl.loop(0, max(reach, last))
     def _(step):
-        finish_wrap(step)
+        @pl.when(step < reach)
+        def _():
+            finish_down(step, True)
+
+        @pl.when(step > reach)
+        def _():
+            finish_wrap(step)
 
     @pl.loop(0, n - 1)
     def _(i):
@@ -513,14 +534,6 @@
     dk_out[0] = grad.astype(BF16)
     dv_out[0] = keep[reach, 0, 1, core].astype(BF16)
 
-    @pl.loop(0, group - 1)
-    def _(i):
-        plane_copy(i, (place + offset(i, group)) % group).wait_recv()
-
-    q_total = jnp.sum(plane_in[...], axis=0)
-    gains_out[0:1] = q_total
-    gains_out[1:2] = q_total * q_gain[...] / k_gain[...]
-
     def left(copy):
         copy.wait_send()
 
@@ -557,11 +570,19 @@
     def _(i):
         line_copy(i, me).wait_send()
 
+    store.wait()
+
+    @pl.loop(0, group - 1)
+    def _(i):
+        plane_copy(i, (place + offset(i, group)) % group).wait_recv()
+
+    q_total = jnp.sum(plane_in[...], axis=0)
+    gains_out[0:1] = q_total
+    gains_out[1:2] = q_total * q_gain[...] / k_gain[...]
+
     @pl.loop(0, group - 1)
     def _(i):
         plane_copy(i, place).wait_send()
-
-    store.wait()
 
 
 def hand_over(*refs):

time: 83.5 us -> 78.9 us (0.945)
  Pallas kernels: 82.7 us -> 78.1 us
    pallas_call x1, Pallas kernels: 81 us -> 76.4 us  [shards(): pl.pallas_call(functools.partial(kernel, n, tp, dp), out_shape=(jax.Shape...]
where the time goes in v4:
time: 78.9 us; the launch traced here: 78.7 us
  Pallas kernels  78.1 us (99%)
    pallas_call x1, Pallas kernels, shards(): pl.pallas_call(functools.partial(kernel, n, tp, dp), out_shape=(jax.Shape...  76.4 us
    pallas_call x1, Pallas kernels, shards(): pl.pallas_call(hand_over, out_shape=tuple((jax.ShapeDtypeStruct(x.shape,...  1.7 us

profile of v4, /device:TPU:1, one launch (start us, length us, event | category | flops | bytes accessed | tf_op | source)
XLA Modules:
  0.0 78.7 jit_solution(12269876677552236837)
XLA Ops:
  0.6 76.4 %shard_map.93 = (bf16[1,128,1024]{2,1,0:T(8,128)(2,1)}, bf16[1,128,128]{2,1,0:T(8,128)(2,1)}, bf16[1,128,128]{2,1,0:T(8,128)(2,1)}, f32[2,128]{1,0:T(2,128)}) custom-call(bf16[1,128,1024]{2,1,0:T(8,128)(2,1)} %q_hbm.1, bf16[1,128,128]{2,1,0:T(8,128)(2,1)} %k_hbm.1, bf16[1,128,128]{2,1,0:T(8,128)(2,1)} %v_hbm.1, bf16[1,128,1024]{2,1,0:T(8,128)(2,1)} %g_hbm.1, ...), custom_call_target="tpu_custom_call" | custom-call | flops 5368709120 | bytes 786432 | tf_op jit(solution)/shard_map/pallas_call | solution.py:605
  77.0 1.7 %shard_map.94 = (bf16[1,128,1024]{2,1,0:T(8,128)(2,1)}, bf16[1,128,128]{2,1,0:T(8,128)(2,1)}, bf16[1,128,128]{2,1,0:T(8,128)(2,1)}, f32[2,128]{1,0:T(2,128)}) custom-call(bf16[1,128,1024]{2,1,0:T(8,128)(2,1)} %get-tuple-element.8.refs_0_, bf16[1,128,128]{2,1,0:T(8,128)(2,1)} %get-tuple-element.9.refs_1_, bf16[1,128,128]{2,1,0:T(8,128)(2,1)} %get-tuple-element.10.refs_2_, ...), custom_call_target="tpu_custom_call" | custom-call | tf_op jit(solution)/shard_map/pallas_call | solution.py:658

commit v5 on v4

--- a/solution.py
+++ b/solution.py
@@ -9,18 +9,18 @@
 from jax.sharding import PartitionSpec as P
 
 HD = 128
-CW = 256
+CW = 512
 EPS = 1e-06
 MASKED = -1e30
 F32 = jnp.float32
 BF16 = jnp.bfloat16
 MESH = pl.DeviceIdType.MESH
 
-GATHER = {0: (1, 3), 1: (2,), 3: (4, 6), 4: (5,), 6: (7, 8)}
+GATHER = {0: (1, 2), 2: (3, 4), 4: (5, 6), 6: (7, 8)}
 SCATTER = {0: (1, 3), 1: (2,), 3: (4, 6), 4: (5,), 6: (7, 8)}
 AROUND = {0: (1, 3), 1: (2,), 3: (4, 6), 4: (5,)}
 WRAP = {0: (1, 3), 1: (2,), 3: (4, 5, 6)}
-GATHER_ORDER = (1, 3, 2, 4, 6, 5, 7, 8)
+GATHER_ORDER = (2, 1, 4, 3, 6, 5, 8, 7)
 SCATTER_ORDER = (8, 7, 5, 2, 6, 4, 1, 3)
 AROUND_DELAY = {0: 0, 1: 2, 3: 2, 2: 4, 4: 4, 6: 4, 5: 5}
 WRAP_UP = False
@@ -33,6 +33,10 @@
     for key, value in table.items():
         out = jnp.where(index == key, value, out)
     return out
+
+
+def around_ring(index, size):
+    return jnp.where(index >= size, index - size, index)
 
 
 def children(tree, reach, slot):
@@ -222,9 +226,11 @@
             def _():
                 act(up_copy(z - distance, child, part, to))
 
+    around_children = [pick(below_top, children(AROUND, far, slot)) for slot in range(2)]
+
     def each_around_send(owner, part, act):
         for slot in (1, 0):
-            child = pick(below_top, children(AROUND, far, slot))
+            child = around_children[slot]
 
             @pl.when(jnp.logical_and(child > 0, owner <= far - child))
             def _():
@@ -375,9 +381,12 @@
                 down_copy(child, part, z).wait_recv()
                 keep[step, 0, part, core] += down_in[child, part].astype(F32)
 
+    wrap_children = [pick(below_top, children(WRAP, far, slot)) for slot in range(3)]
+    my_slot, my_parent = pick(below_top, wrap_slot), pick(below_top, wrap_parent)
+
     def add_wrap(step, owner, part):
         for slot in range(3):
-            child = pick(below_top, children(WRAP, far, slot))
+            child = wrap_children[slot]
 
             @pl.when(jnp.logical_and(child > 0, owner <= far - child))
             def _():
@@ -389,9 +398,9 @@
 
     def each_wrap_send(owner, part, act):
         for slot in range(3):
-            @pl.when(pick(below_top, wrap_slot) == slot)
-            def _():
-                act(wrap_copy(owner, slot, part, top - pick(below_top, wrap_parent)))
+            @pl.when(my_slot == slot)
+            def _():
+                act(wrap_copy(owner, slot, part, top - my_parent))
 
         @pl.when(below_top == 0)
         def _():
@@ -423,8 +432,12 @@
                     down_out[distance, part] = both.astype(BF16)
                 down_copy(distance, part, to).start()
 
-    heights = {p * chips + e: height(p, e, far) for p in range(far + 1) for e in range(far - p + 1)}
+    heights = {(p, e): height(p, e, far) for p in range(far + 1) for e in range(far - p + 1)}
     tallest = max(heights.values())
+    limits = []
+    for least in range(1, tallest + 1):
+        waits = {p: max((e for (q, e), h in heights.items() if q == p and h >= least), default=-1) for p, _ in heights}
+        limits.append(pick(below_top, {p: e for p, e in waits.items() if e >= 0}))
 
     def finish_wrap(now):
         @pl.loop(0, tallest + 1)
@@ -432,7 +445,11 @@
             step = now - WRAP_LAG[0] - WRAP_LAG[1] * tall
             owner, valid = owed(1, step)
 
-            @pl.when(jnp.logical_and(valid, pick(below_top * chips + owner, heights) == tall))
+            waits = jnp.int32(0)
+            for limit in limits:
+                waits += jnp.where(owner <= limit, 1, 0)
+
+            @pl.when(jnp.logical_and(valid, waits == tall))
             def _():
                 add_swapped(step, 1, owner)
                 for part in range(2):
@@ -480,13 +497,13 @@
     def line_copy(i, slot):
         return pltpu.make_async_remote_copy(
             line_out, line_in.at[slot], line_send.at[i], line_recv.at[slot],
-            device_id={"ctx": (me + offset(i, n)) % n}, device_id_type=MESH,
+            device_id={"ctx": around_ring(me + offset(i, n), n)}, device_id_type=MESH,
         )
 
     def plane_copy(i, slot):
         return pltpu.make_async_remote_copy(
             plane_out, plane_in.at[slot], plane_send.at[i], plane_recv.at[slot],
-            device_id=plane((place + offset(i, group)) % group), device_id_type=MESH,
+            device_id=plane(around_ring(place + offset(i, group), group)), device_id_type=MESH,
         )
 
     line_out[...] = q_part
@@ -509,7 +526,7 @@
 
     @pl.loop(0, n - 1)
     def _(i):
-        line_copy(i, (me + offset(i, n)) % n).wait_recv()
+        line_copy(i, around_ring(me + offset(i, n), n)).wait_recv()
 
     plane_out[...] = jnp.sum(line_in[...], axis=0)
     plane_in[place] = plane_out[...]
@@ -574,7 +591,7 @@
 
     @pl.loop(0, group - 1)
     def _(i):
-        plane_copy(i, (place + offset(i, group)) % group).wait_recv()
+        plane_copy(i, around_ring(place + offset(i, group), group)).wait_recv()
 
     q_total = jnp.sum(plane_in[...], axis=0)
     gains_out[0:1] = q_total

time: 78.9 us -> 77 us (0.976)
  Pallas kernels: 78.1 us -> 76.2 us
    pallas_call x1, Pallas kernels: 76.4 us -> 74.5 us  [shards(): pl.pallas_call(functools.partial(kernel, n, tp, dp), out_shape=(jax.Shape...]
where the time goes in v5:
time: 77 us; the launch traced here: 76.8 us
  Pallas kernels  76.2 us (99%)
    pallas_call x1, Pallas kernels, shards(): pl.pallas_call(functools.partial(kernel, n, tp, dp), out_shape=(jax.Shape...  74.5 us
    pallas_call x1, Pallas kernels, shards(): pl.pallas_call(hand_over, out_shape=tuple((jax.ShapeDtypeStruct(x.shape,...  1.7 us

profile of v5, /device:TPU:1, one launch (start us, length us, event | category | flops | bytes accessed | tf_op | source)
XLA Modules:
  0.0 76.8 jit_solution(4111553749570893328)
XLA Ops:
  0.6 74.5 %shard_map.93 = (bf16[1,128,1024]{2,1,0:T(8,128)(2,1)}, bf16[1,128,128]{2,1,0:T(8,128)(2,1)}, bf16[1,128,128]{2,1,0:T(8,128)(2,1)}, f32[2,128]{1,0:T(2,128)}) custom-call(bf16[1,128,1024]{2,1,0:T(8,128)(2,1)} %q_hbm.1, bf16[1,128,128]{2,1,0:T(8,128)(2,1)} %k_hbm.1, bf16[1,128,128]{2,1,0:T(8,128)(2,1)} %v_hbm.1, bf16[1,128,1024]{2,1,0:T(8,128)(2,1)} %g_hbm.1, ...), custom_call_target="tpu_custom_call" | custom-call | flops 5368709120 | bytes 786432 | tf_op jit(solution)/shard_map/pallas_call | solution.py:622
  75.1 1.7 %shard_map.94 = (bf16[1,128,1024]{2,1,0:T(8,128)(2,1)}, bf16[1,128,128]{2,1,0:T(8,128)(2,1)}, bf16[1,128,128]{2,1,0:T(8,128)(2,1)}, f32[2,128]{1,0:T(2,128)}) custom-call(bf16[1,128,1024]{2,1,0:T(8,128)(2,1)} %get-tuple-element.8.refs_0_, bf16[1,128,128]{2,1,0:T(8,128)(2,1)} %get-tuple-element.9.refs_1_, bf16[1,128,128]{2,1,0:T(8,128)(2,1)} %get-tuple-element.10.refs_2_, ...), custom_call_target="tpu_custom_call" | custom-call | tf_op jit(solution)/shard_map/pallas_call | solution.py:675

commit v6 on v5

--- a/solution.py
+++ b/solution.py
@@ -483,35 +483,38 @@
     for h in range(heads):
         cols = slice(h * HD, (h + 1) * HD)
         x = q_raw[:, cols].astype(F32)
-        upstream = scale * dq_t[:, cols].T
-        grad, part = norm_back(x, inverse_rms(x), q_gain[...], upstream)
-        q_part += part
+        q_part += jnp.sum(scale * dq_t[:, cols].T * x * inverse_rms(x), axis=0, keepdims=True)
+
+    def offset(i, count):
+        away = (i + 1) // 2
+        return count // 2 + jnp.where(i % 2 == 1, -away, away)
+
+    def line_copy(i, slot):
+        return pltpu.make_async_remote_copy(
+            line_out, line_in.at[slot], line_send.at[i], line_recv.at[slot],
+            device_id={"ctx": around_ring(me + offset(i, n), n)}, device_id_type=MESH,
+        )
+
+    def plane_copy(i, slot):
+        return pltpu.make_async_remote_copy(
+            plane_out, plane_in.at[slot], plane_send.at[i], plane_recv.at[slot],
+            device_id=plane(around_ring(place + offset(i, group), group)), device_id_type=MESH,
+        )
+
+    line_out[...] = q_part
+    line_in[me] = q_part
+
+    @pl.loop(0, n - 1)
+    def _(i):
+        line_copy(i, me).start()
+
+    for h in range(heads):
+        cols = slice(h * HD, (h + 1) * HD)
+        x = q_raw[:, cols].astype(F32)
+        grad, _ = norm_back(x, inverse_rms(x), q_gain[...], scale * dq_t[:, cols].T)
         dq_out[:, cols] = grad.astype(BF16)
     store = pltpu.make_async_copy(dq_out, dq_hbm.at[0], store_sem)
     store.start()
-
-    def offset(i, count):
-        away = (i + 1) // 2
-        return count // 2 + jnp.where(i % 2 == 1, -away, away)
-
-    def line_copy(i, slot):
-        return pltpu.make_async_remote_copy(
-            line_out, line_in.at[slot], line_send.at[i], line_recv.at[slot],
-            device_id={"ctx": around_ring(me + offset(i, n), n)}, device_id_type=MESH,
-        )
-
-    def plane_copy(i, slot):
-        return pltpu.make_async_remote_copy(
-            plane_out, plane_in.at[slot], plane_send.at[i], plane_recv.at[slot],
-            device_id=plane(around_ring(place + offset(i, group), group)), device_id_type=MESH,
-        )
-
-    line_out[...] = q_part
-    line_in[me] = q_part
-
-    @pl.loop(0, n - 1)
-    def _(i):
-        line_copy(i, me).start()
 
     last = far + 1 + WRAP_LAG[0] + WRAP_LAG[1] * tallest
     @pl.loop(0, max(reach, last))

time: 77 us -> 76.9 us (level)
  no operation moved by 1% of the time
where the time goes in v6:
time: 76.9 us; the launch traced here: 76.7 us
  Pallas kernels  76.1 us (99%)
    pallas_call x1, Pallas kernels, shards(): pl.pallas_call(functools.partial(kernel, n, tp, dp), out_shape=(jax.Shape...  74.4 us
    pallas_call x1, Pallas kernels, shards(): pl.pallas_call(hand_over, out_shape=tuple((jax.ShapeDtypeStruct(x.shape,...  1.7 us

profile of v6, /device:TPU:1, one launch (start us, length us, event | category | flops | bytes accessed | tf_op | source)
XLA Modules:
  0.0 76.7 jit_solution(9372821674270236332)
XLA Ops:
  0.6 74.4 %shard_map.93 = (bf16[1,128,1024]{2,1,0:T(8,128)(2,1)}, bf16[1,128,128]{2,1,0:T(8,128)(2,1)}, bf16[1,128,128]{2,1,0:T(8,128)(2,1)}, f32[2,128]{1,0:T(2,128)}) custom-call(bf16[1,128,1024]{2,1,0:T(8,128)(2,1)} %q_hbm.1, bf16[1,128,128]{2,1,0:T(8,128)(2,1)} %k_hbm.1, bf16[1,128,128]{2,1,0:T(8,128)(2,1)} %v_hbm.1, bf16[1,128,1024]{2,1,0:T(8,128)(2,1)} %g_hbm.1, ...), custom_call_target="tpu_custom_call" | custom-call | flops 5368709120 | bytes 786432 | tf_op jit(solution)/shard_map/pallas_call | solution.py:625
  75.0 1.7 %shard_map.94 = (bf16[1,128,1024]{2,1,0:T(8,128)(2,1)}, bf16[1,128,128]{2,1,0:T(8,128)(2,1)}, bf16[1,128,128]{2,1,0:T(8,128)(2,1)}, f32[2,128]{1,0:T(2,128)}) custom-call(bf16[1,128,1024]{2,1,0:T(8,128)(2,1)} %get-tuple-element.8.refs_0_, bf16[1,128,128]{2,1,0:T(8,128)(2,1)} %get-tuple-element.9.refs_1_, bf16[1,128,128]{2,1,0:T(8,128)(2,1)} %get-tuple-element.10.refs_2_, ...), custom_call_target="tpu_custom_call" | custom-call | tf_op jit(solution)/shard_map/pallas_call | solution.py:678
